TPU v7x, 256 devices: a whole 4x4x8 slice. The times are simulated.
256 devices in a mesh: pipe: 2 (over x_lo), ctx: 16 (over x_hi, z), tp: 8 (over y, core).
Axes of the slice: x: 4 (x_hi: 2, x_lo: 2; x = x_hi * 2 + x_lo), y: 4, z: 8, core: 2. Of those that a mesh axis runs over, the one named last changes fastest.
Arguments:
- fwd_queries: bfloat16 [2, 2048, 8192], P('pipe', 'ctx', 'tp'), may hold values from -6 to 6
- fwd_keyvals: bfloat16 [2, 2, 2048, 1024], P('pipe', None, 'ctx', 'tp'), may hold values from -6 to 6
- bwd_queries: bfloat16 [2, 2048, 8192], P('pipe', 'ctx', 'tp'), may hold values from -6 to 6
- bwd_keyvals: bfloat16 [2, 2, 2048, 1024], P('pipe', None, 'ctx', 'tp'), may hold values from -6 to 6
- bwd_cotangent: bfloat16 [2, 2048, 8192], P('pipe', 'ctx', 'tp'), may hold values from -6 to 6
- doc_lengths: int32 [2, 8], replicated, may hold values from 1 to 1024, 2048 in all within a row
- block_order: int32 [2, 16], replicated, may hold values from 0 to 15, each once within a row
Outputs:
- arrived_output: bfloat16 [2, 2048, 8192], P('pipe', 'ctx', 'tp')
- arrived_query_grad: bfloat16 [2, 2048, 8192], P('pipe', 'ctx', 'tp')
- arrived_keyval_grad: bfloat16 [2, 2, 2048, 1024], P('pipe', None, 'ctx', 'tp')
Inputs may be any that keep to these rules, and one draw needn't show every extreme that they name: `block_order`: each row is a permutation of 0 to 15. `doc_lengths`: each row sums to 2048.
All inputs are finite; a program needn't handle non-finite values.
Results may differ from a plain program's by a relative error of at most 0.023.
Values may be sent and summed in bfloat16 or wider, within the bound.
No kernel may reach another device: no remote copies, remote signals or barrier semaphores. Data moves between devices by JAX's collectives and lax.ppermute only.
A program may use at most 64 MiB of HBM per device.

v0:
```python
import jax
import jax.numpy as jnp
from jax import lax
from jax.sharding import PartitionSpec as P

HEADS = 64
KVH = 8
HD = 128
BLOCK = 128


NEG = -1e30


def from_behind(block, axis, distance):
    devices = range(lax.axis_size(axis))
    route = [((i - distance) % len(devices), i) for i in devices]
    return lax.ppermute(block, axis, route)


def layout(order, lengths):
    starts = jnp.repeat(order * BLOCK, BLOCK, total_repeat_length=order.shape[0] * BLOCK)
    offsets = jnp.tile(jnp.arange(BLOCK, dtype=jnp.int32), order.shape[0])
    position = starts + offsets
    ends = jnp.cumsum(lengths)
    document = jnp.sum((position[:, None] >= ends[None, :]).astype(jnp.int32), axis=1)
    return (position, document)


def piece_scores(query, piece, start, context):
    position, document, query_pos, query_doc = context
    count = piece.shape[1]
    kv_dev = query.shape[1]
    key = piece[0].reshape(count, kv_dev, HD)
    value = piece[1].reshape(count, kv_dev, HD)
    scores = jnp.einsum("qhgd,khd->hgqk", query, key, preferred_element_type=jnp.float32) * HD ** (
        -0.5
    )
    key_pos = lax.dynamic_slice_in_dim(position, start, count)
    key_doc = lax.dynamic_slice_in_dim(document, start, count)
    mask = (key_doc[None, :] == query_doc[:, None]) & (key_pos[None, :] <= query_pos[:, None])
    mask = mask[None, None]
    scores = jnp.where(mask, scores, NEG)
    return (scores, mask, key, value)


def make_stats(query, context, carry, piece, start):
    top, total, acc = carry
    scores, mask, key, value = piece_scores(query, piece, start, context)
    new_top = jnp.maximum(top, jnp.max(scores, axis=-1))
    factor = jnp.exp(top - new_top)
    probs = jnp.where(mask, jnp.exp(scores - new_top[..., None]), 0.0)
    total = total * factor + jnp.sum(probs, axis=-1)
    update = jnp.einsum(
        "hgqk,khd->hgqd", probs.astype(jnp.bfloat16), value, preferred_element_type=jnp.float32
    )
    acc = acc * factor[..., None] + update
    return (new_top, total, acc)


def make_grads(query, cotan, lse, delta, context, carry, piece, start):
    query_grad, keyval_grad = carry
    count = piece.shape[1]
    scores, mask, key, value = piece_scores(query, piece, start, context)
    probs = jnp.where(mask, jnp.exp(scores - lse[..., None]), 0.0)
    value_grad = jnp.einsum(
        "hgqk,qhgd->khd", probs.astype(jnp.bfloat16), cotan, preferred_element_type=jnp.float32
    )
    dprobs = jnp.einsum("qhgd,khd->hgqk", cotan, value, preferred_element_type=jnp.float32)
    dscores = (probs * (dprobs - delta[..., None])).astype(jnp.bfloat16)
    query_grad = query_grad + jnp.einsum(
        "hgqk,khd->hgqd", dscores, key, preferred_element_type=jnp.float32
    ) * HD ** (-0.5)
    key_grad = jnp.einsum(
        "hgqk,qhgd->khd", dscores, query, preferred_element_type=jnp.float32
    ) * HD ** (-0.5)
    fresh = jnp.stack([key_grad.reshape(count, -1), value_grad.reshape(count, -1)])
    before = keyval_grad
    keyval_grad = before + fresh
    return (query_grad, keyval_grad)


def shards(
    fwd_queries, fwd_keyvals, bwd_queries, bwd_keyvals, bwd_cotangent, doc_lengths, block_order
):
    rows = fwd_queries.shape[1]
    ctx_count = lax.axis_size("ctx")
    whole_len = rows * ctx_count
    first_row = lax.axis_index("ctx") * rows
    kv_dev = fwd_keyvals.shape[3] // HD
    group = HEADS // KVH

    def prepare(queries, batch):
        position, document = layout(block_order[batch], doc_lengths[batch])
        query_pos = lax.dynamic_slice_in_dim(position, first_row, rows)
        query_doc = lax.dynamic_slice_in_dim(document, first_row, rows)
        query = queries[0].reshape(rows, kv_dev, group, HD)
        return (query, (position, document, query_pos, query_doc))

    def stats_init():
        top = jnp.full((kv_dev, group, rows), NEG, jnp.float32)
        total = jnp.zeros((kv_dev, group, rows), jnp.float32)
        acc = jnp.zeros((kv_dev, group, rows, HD), jnp.float32)
        return (top, total, acc)

    def flatten(values):
        return values.transpose(2, 0, 1, 3).reshape(rows, kv_dev * group * HD)

    query, context = prepare(fwd_queries, 1)
    top, total, acc = make_stats(
        query,
        context,
        stats_init(),
        lax.all_gather(fwd_keyvals[0], "ctx", axis=1, tiled=True),
        jnp.int32(0),
    )
    output = flatten(acc / total[..., None]).astype(jnp.bfloat16)[None]
    query, context = prepare(bwd_queries, 0)
    cotan = bwd_cotangent[0].reshape(rows, kv_dev, group, HD)
    grad_init = (
        jnp.zeros((kv_dev, group, rows, HD), jnp.float32),
        jnp.zeros((2, whole_len, kv_dev * HD), jnp.float32),
    )
    stats = make_stats(
        query,
        context,
        stats_init(),
        lax.all_gather(bwd_keyvals[0], "ctx", axis=1, tiled=True),
        jnp.int32(0),
    )
    top, total, acc = stats
    outcome = acc / total[..., None]
    lse = top + jnp.log(total)
    delta = jnp.einsum("qhgd,hgqd->hgq", cotan, outcome, preferred_element_type=jnp.float32)
    lse, delta = (lse, delta)
    query_grad, keyval_grad = make_grads(
        query,
        cotan,
        lse,
        delta,
        context,
        grad_init,
        lax.all_gather(bwd_keyvals[0], "ctx", axis=1, tiled=True),
        jnp.int32(0),
    )
    own_keyval = lax.psum_scatter(
        keyval_grad.astype(jnp.bfloat16), "ctx", scatter_dimension=1, tiled=True
    )
    query_out = flatten(query_grad).astype(jnp.bfloat16)[None]
    keyval_out = own_keyval[None]
    arrived_output = from_behind(output, "pipe", 1)
    arrived_query_grad, arrived_keyval_grad = from_behind((query_out, keyval_out), "pipe", -1)
    return (arrived_output, arrived_query_grad, arrived_keyval_grad)


def solution(mesh):
    placed = (
        P("pipe", "ctx", "tp"),
        P("pipe", None, "ctx", "tp"),
        P("pipe", "ctx", "tp"),
        P("pipe", None, "ctx", "tp"),
        P("pipe", "ctx", "tp"),
        P(),
        P(),
    )
    return jax.shard_map(
        shards,
        mesh=mesh,
        in_specs=placed,
        out_specs=(P("pipe", "ctx", "tp"), P("pipe", "ctx", "tp"), P("pipe", None, "ctx", "tp")),
        check_vma=False,
    )
```

profile of v0, /device:TPU:8, one launch (start us, length us, event | category | flops | bytes accessed | tf_op | source)
XLA Modules:
  0.0 399.3 jit_solution(3111465387119964873)
XLA Ops:
  7.2 0.7 all-gather.5.cloned.1.call-update
  7.9 0.7 all-gather.7.cloned.1.call-update
  8.6 0.0 reduce-scatter.2.cloned.1.call-start
  8.7 0.8 multiply_bitcast_fusion
  9.5 0.7 fusion.104
  10.2 0.8 slice_bitcast_fusion.10
  10.9 0.2 reduce-window.20
  11.1 10.0 %bitcast_add_fusion.1 = s32[2048]{0:T(1024)S(1)} fusion(s32[]{:T(128)} %bitcast.18, s32[]{:T(128)} %bitcast.17, s32[]{:T(128)} %bitcast.16, s32[]{:T(128)} %bitcast.15, s32[]{:T(128)} %bitcast.14, s32[]{:T(128)} %bitcast.13, s32[]{:T(128)} %bitcast.12, s32[]{:T(128)} %bitcast.11, s32[]{:T(128)} %bitcast.10, s32[]{:T(128)} %bitcast.9, s32[]{:T(128)} %bitcast.8, ...), kind=kLoop, calls=%fused_computation.61 | loop fusion | flops 81920 | bytes 8256 | tf_op jit(solution)/shard_map/add | solution.py:24
  21.2 0.1 convert_reduce_fusion.1
  21.3 0.1 dynamic_slice.13
  21.3 0.1 dynamic_slice.12
  21.4 1.0 copy.44
  22.4 0.7 fusion.103
  23.1 10.0 %bitcast_add_fusion = s32[2048]{0:T(1024)S(1)} fusion(s32[]{:T(128)} %bitcast.48, s32[]{:T(128)} %bitcast.47, s32[]{:T(128)} %bitcast.46, s32[]{:T(128)} %bitcast.45, s32[]{:T(128)} %bitcast.44, s32[]{:T(128)} %bitcast.43, s32[]{:T(128)} %bitcast.42, s32[]{:T(128)} %bitcast.41, s32[]{:T(128)} %bitcast.40, s32[]{:T(128)} %bitcast.39, s32[]{:T(128)} %bitcast.38, ...), kind=kLoop, calls=%fused_computation.60 | loop fusion | flops 81920 | bytes 8256 | tf_op jit(solution)/shard_map/add | solution.py:24
  33.2 0.1 dynamic_slice.15
  33.3 0.2 reduce-window.21
  33.5 0.1 convert_reduce_fusion
  33.6 0.1 dynamic_slice.14
  33.6 1.0 copy.45
  34.6 1.0 copy.46
  35.6 1.3 compare_and_fusion.1
  37.0 1.3 compare_and_fusion
  38.3 54.1 %all-gather.5.cloned.1.call-done = bf16[1,2,2048,128]{3,2,1,0:T(8,128)(2,1)} async-done(((bf16[1,2,128,128]{3,2,1,0:T(8,128)(2,1)}), bf16[1,2,2048,128]{3,2,1,0:T(8,128)(2,1)}) %all-gather.5.cloned.1.call-update) | async-done | bytes 1048592 | tf_op jit(solution)/shard_map/all_gather | solution.py:114
  92.4 5.6 %fusion.2 = (f32[8,128]{1,0:T(8,128)S(1)}, f32[2048,128,8]{1,0,2:T(8,128)}) fusion(pred[128,2048]{0,1:T(8,128)(4,1)S(1)} %compare_and_fusion.1, bf16[128,8,128]{2,1,0:T(8,128)(2,1)S(1)} %bitcast.335, bf16[1,2,2048,128]{3,2,1,0:T(8,128)(2,1)} %all-gather.5.cloned.1.call-done), kind=kOutput, calls=%fused_computation.8 | convolution fusion | flops 543161344 | bytes 9441280 | tf_op jit(solution)/shard_map/qhgd,khd->hgqk/dot_general | solution.py:36
  98.1 72.5 %all-gather.7.cloned.1.call-done = bf16[1,2,2048,128]{3,2,1,0:T(8,128)(2,1)} async-done(((bf16[1,2,128,128]{3,2,1,0:T(8,128)(2,1)}), bf16[1,2,2048,128]{3,2,1,0:T(8,128)(2,1)}) %all-gather.7.cloned.1.call-update) | async-done | bytes 1048592 | tf_op jit(solution)/shard_map/all_gather | solution.py:143
  170.5 2.5 fusion.8
  173.0 2.0 fusion.4
  175.1 2.5 fusion.58
  177.6 0.4 multiply_reduce_fusion
  178.0 5.5 %fusion.43 = bf16[1,2048,128]{2,1,0:T(8,128)(2,1)S(1)} fusion(f32[2048,128,8]{1,0,2:T(8,128)} %copy-done, f32[8,128]{1,0:T(8,128)S(1)} %get-tuple-element.24, pred[128,2048]{0,1:T(8,128)(4,1)S(1)} %compare_and_fusion, bf16[128,8,128]{2,1,0:T(8,128)(2,1)S(1)} %bitcast.330), kind=kOutput, calls=%fused_computation.34 | convolution fusion | flops 547618816 | bytes 9441280 | tf_op jit(solution)/shard_map/hgqk,qhgd->khd/dot_general | solution.py:66
  183.6 0.2 copy-done.1
  183.8 3.2 fusion.1
  187.1 1.3 fusion.40
  188.3 0.7 copy-done.4
  189.0 1.1 pad_maximum_fusion
  190.2 4.5 %fusion.6 = f32[8,128]{1,0:T(8,128)S(1)} fusion(f32[2048,128,8]{1,0,2:T(8,128)} %get-tuple-element.66, f32[8,128]{1,0:T(8,128)S(1)} %broadcast_maximum_fusion.1, pred[128,2048]{0,1:T(8,128)(4,1)S(1)} %compare_and_fusion.1), kind=kLoop, calls=%fused_computation.12 | loop fusion | flops 10484736 | bytes 8658944 | tf_op jit(solution)/shard_map/reduce_sum | solution.py:53
  194.7 5.5 %fusion.64 = bf16[8,128,128]{1,2,0:T(8,128)(2,1)S(1)} fusion(f32[2048,128,8]{1,0,2:T(8,128)} %get-tuple-element.66, f32[8,128]{1,0:T(8,128)S(1)} %broadcast_maximum_fusion.1, pred[128,2048]{0,1:T(8,128)(4,1)S(1)} %compare_and_fusion.1, bf16[1,2,2048,128]{3,2,1,0:T(8,128)(2,1)S(1)} %copy-done.3, f32[8,128]{1,0:T(8,128)S(1)} %get-tuple-element.28, ...), kind=kOutput, calls=%fused_computation.44 | convolution fusion | flops 547749888 | bytes 9449472 | tf_op jit(solution)/shard_map/hgqk,khd->hgqd/dot_general | solution.py:54
  200.2 0.1 copy.24
  200.3 0.7 collective-permute-start
  201.0 3.0 fusion.55
  204.0 0.1 copy.29
  204.1 1.5 collective-permute-start.1
  205.7 180.6 %reduce-scatter.2.cloned.1.call-done = bf16[2,128,128]{2,1,0:T(8,128)(2,1)} async-done(((bf16[2,2048,128]{2,1,0:T(8,128)(2,1)}), bf16[2,128,128]{2,1,0:T(8,128)(2,1)}) %reduce-scatter.2.cloned.1.call-update) | async-done | bytes 65552 | tf_op jit(solution)/shard_map/reduce_scatter | solution.py:146
  386.2 0.6 collective-permute-start.2
  386.8 3.9 collective-permute-done.2
  390.7 0.7 copy.65
  391.4 0.7 copy.66
  392.1 0.6 copy.67
  (18 shorter events, 0.2 us)
Async XLA Ops:
  7.2 85.3 %all-gather.5.cloned.1.call-start = ((), (), s32[]{:S(2)}) async-start(), calls=%async_computation.2 | async-start | bytes 1114112 | tf_op jit(solution)/shard_map/all_gather | solution.py:114
  7.9 162.6 %all-gather.7.cloned.1.call-start = ((), (), s32[]{:S(2)}) async-start(), calls=%async_computation.3 | async-start | bytes 1114112 | tf_op jit(solution)/shard_map/all_gather | solution.py:143
  8.6 377.6 %reduce-scatter.2.cloned.1.call-start = ((), (), s32[]{:S(2)}) async-start(), calls=%async_computation.1 | async-start | bytes 1114112 | tf_op jit(solution)/shard_map/reduce_scatter | solution.py:146
  170.5 4.6 %copy-start.2 = (bf16[1,2,2048,128]{3,2,1,0:T(8,128)(2,1)S(1)}, bf16[1,2,2048,128]{3,2,1,0:T(8,128)(2,1)}, u32[]{:S(2)}) copy-start(bf16[1,2,2048,128]{3,2,1,0:T(8,128)(2,1)} %all-gather.7.cloned.1.call-done) | copy-start | bytes 3145732
  173.0 4.6 %copy-start = (f32[2048,128,8]{1,0,2:T(8,128)}, f32[2048,128,8]{1,0,2:T(8,128)S(1)}, u32[]{:S(2)}) copy-start(f32[2048,128,8]{1,0,2:T(8,128)S(1)} %get-tuple-element.68) | copy-start | bytes 25165828
  178.0 5.8 %copy-start.1 = (f32[2048,128,8]{1,0,2:T(8,128)S(1)}, f32[2048,128,8]{1,0,2:T(8,128)}, u32[]{:S(2)}) copy-start(f32[2048,128,8]{1,0,2:T(8,128)} %copy-done) | copy-start | bytes 25165828
  187.1 2.0 copy-start.4
  187.1 7.6 %copy-start.3 = (bf16[1,2,2048,128]{3,2,1,0:T(8,128)(2,1)S(1)}, bf16[1,2,2048,128]{3,2,1,0:T(8,128)(2,1)}, u32[]{:S(2)}) copy-start(bf16[1,2,2048,128]{3,2,1,0:T(8,128)(2,1)} %all-gather.5.cloned.1.call-done) | copy-start | bytes 3145732
  200.3 186.5 %collective-permute-start = (bf16[1,128,1024]{2,1,0:T(8,128)(2,1)S(1)}, bf16[1,128,1024]{2,1,0:T(8,128)(2,1)S(1)}, u32[]{:S(2)}, u32[]{:S(2)}) collective-permute-start(bf16[1,128,1024]{2,1,0:T(8,128)(2,1)S(1)} %copy.24), channel_id=1, source_target_pairs={{128,0},{0,128},{129,1},{1,129},{130,2},{2,130},{131,3},{3,131},{1... | collective-permute-start | bytes 786440 | tf_op jit(solution)/shard_map/ppermute | solution.py:18
  204.1 182.7 %collective-permute-start.1 = (bf16[1,128,1024]{2,1,0:T(8,128)(2,1)S(1)}, bf16[1,128,1024]{2,1,0:T(8,128)(2,1)S(1)}, u32[]{:S(2)}, u32[]{:S(2)}) collective-permute-start(bf16[1,128,1024]{2,1,0:T(8,128)(2,1)S(1)} %copy.29), channel_id=1, source_target_pairs={{128,0},{0,128},{129,1},{1,129},{130,2},{2,130},{131,3},{3,131},{1... | collective-permute-start | bytes 786440 | tf_op jit(solution)/shard_map/ppermute | solution.py:18
  386.2 4.5 %collective-permute-start.2 = (bf16[1,2,128,128]{3,2,1,0:T(8,128)(2,1)}, bf16[1,2,128,128]{3,2,1,0:T(8,128)(2,1)S(1)}, u32[]{:S(2)}, u32[]{:S(2)}) collective-permute-start(bf16[1,2,128,128]{3,2,1,0:T(8,128)(2,1)} %bitcast.342), channel_id=1, source_target_pairs={{128,0},{0,128},{129,1},{1,129},{130,2},{2,130},{131,3},{3,131},{1... | collective-permute-start | bytes 196616 | tf_op jit(solution)/shard_map/ppermute | solution.py:18
Sparse Core Ops, SparseCore 0:
  10.6 81.7 all-gather.4
  95.0 75.4 all-gather.6
  190.3 195.8 reduce-scatter.1
where the time goes:
time: 400 us; the launch traced here: 399 us
  waiting for transfers between devices  312 us (78%)
  other arithmetic  32.1 us (8%)
  matrix products  29 us (7%)
  between operations  14 us (4%)
  local copies, waits for them, and re-layouts  8.81 us (2%)
    reduce_scatter x1, waiting for transfers between devices, shards(): lax.psum_scatter(keyval_grad.astype(jnp.bfloat16), 'ctx', scatter_dimensi...  181 us
    all_gather x1, waiting for transfers between devices, shards(): lax.all_gather(bwd_keyvals[0], 'ctx', axis=1, tiled=True)  72.5 us
    all_gather x1, waiting for transfers between devices, shards(): lax.all_gather(fwd_keyvals[0], 'ctx', axis=1, tiled=True)  54.1 us
    add x2, other arithmetic, layout(): position = starts + offsets  20.1 us
    dot_general x2, matrix products, piece_scores(): jnp.einsum('qhgd,khd->hgqk', query, key, preferred_element_type=jnp.float32)  8.08 us
  transfers between devices with their start and end apart: 6, of which 4 were waited for; matrix products, arithmetic and copies ran while one was open for 12% of the time, Pallas kernels for 0%

commit v1 on v0

v1 whole, which is shorter than its diff:
```python
import jax
import jax.numpy as jnp
from jax import lax
from jax.experimental import pallas as pl
from jax.experimental.pallas import tpu as pltpu
from jax.sharding import PartitionSpec as P

HD = 128
BLOCK = 128
GROUP = 8
ROWS = GROUP * BLOCK
WIDE = 2 * BLOCK
SLOTS = 16
RING = 8
OFFSETS = (0, -3, 3, -1, -4, 2, 1, -2)
SCALE = HD**-0.5
LOG2E = 1.4426950408889634
NEG = -1e30


def prepare(batch, order, lens, slots, bases):
    me = lax.axis_index("ctx")
    half, z = me // RING, me % RING
    query_base = order[batch, me] * BLOCK
    place = query_base + lax.broadcasted_iota(jnp.int32, (1, BLOCK), 1)
    first = jnp.zeros((1, BLOCK), jnp.int32)
    least = jnp.int32(0)
    end = jnp.int32(0)
    for i in range(lens.shape[1]):
        end = end + lens[batch, i]
        first = jnp.where(place >= end, end, first)
        least = jnp.where(query_base >= end, end, least)
    count = jnp.int32(0)
    for slot in range(SLOTS):
        side = half if slot < RING else 1 - half
        owner = side * RING + (z + (OFFSETS[slot % RING] + RING)) % RING
        base = order[batch, owner] * BLOCK
        slots[count] = slot
        bases[count] = base
        active = (base <= query_base) & (base + (BLOCK - 1) >= least)
        count = count + active.astype(jnp.int32)
    return count, first, place


def dot(a, b):
    return jnp.dot(a, b, preferred_element_type=jnp.float32)


def columns(ref, dst, rows_dst=None):
    for h in range(GROUP):
        part = ref[0, :, h * HD : (h + 1) * HD]
        dst[:, h * BLOCK : (h + 1) * BLOCK] = part.T
        if rows_dst is not None:
            rows_dst[h * BLOCK : (h + 1) * BLOCK, :] = part


def softmax_passes(count, first, place, slots, bases, kv, q_t, probs, acc):
    def scores(i, top):
        slot, base = slots[i], bases[i]
        key = kv[slot, 0]
        row = base + lax.broadcasted_iota(jnp.int32, (BLOCK, BLOCK), 0)
        mask = (row >= first) & (row <= place)
        tops = []
        for c in range(ROWS // WIDE):
            s = dot(key, q_t[:, c * WIDE : (c + 1) * WIDE])
            for j in range(WIDE // BLOCK):
                part = jnp.where(mask, s[:, j * BLOCK : (j + 1) * BLOCK], NEG)
                at = c * WIDE + j * BLOCK
                probs[i, :, at : at + BLOCK] = part
                tops.append(jnp.max(part.reshape(BLOCK // 8, 8, BLOCK), axis=0))
        return jnp.maximum(top, jnp.concatenate(tops, axis=1))

    top = lax.fori_loop(0, count, scores, jnp.full((8, ROWS), NEG, jnp.float32))
    top = jnp.max(top, axis=0, keepdims=True)
    acc[...] = jnp.zeros_like(acc)

    def sums(i, total):
        value_t = kv[slots[i], 1].T
        totals = []
        for c in range(ROWS // WIDE):
            at = slice(c * WIDE, (c + 1) * WIDE)
            p = jnp.exp2((probs[i, :, at] - top[:, at]) * (SCALE * LOG2E))
            probs[i, :, at] = p
            totals.append(jnp.sum(p.reshape(BLOCK // 8, 8, WIDE), axis=0))
            acc[:, at] += dot(value_t, p.astype(jnp.bfloat16))
        return total + jnp.concatenate(totals, axis=1)

    total = lax.fori_loop(0, count, sums, jnp.zeros((8, ROWS), jnp.float32))
    return jnp.sum(total, axis=0, keepdims=True)


def forward_kernel(order, lens, q, near, far, out, slots, bases, kv, q_t, probs, acc):
    count, first, place = prepare(1, order, lens, slots, bases)
    columns(q, q_t)
    kv[:RING] = near[...]
    kv[RING:] = far[...]
    total = softmax_passes(count, first, place, slots, bases, kv, q_t, probs, acc)
    inverse = 1.0 / total
    for h in range(GROUP):
        at = slice(h * BLOCK, (h + 1) * BLOCK)
        out[0, :, at] = (acc[:, at] * inverse[:, at]).T.astype(jnp.bfloat16)


def backward_kernel(
    order, lens, q, cotan, near, far, dq, dnear, dfar,
    slots, bases, kv, q_t, c_t, q_rows, c_rows, probs, acc, dkv,
):
    count, first, place = prepare(0, order, lens, slots, bases)
    columns(q, q_t, q_rows)
    columns(cotan, c_t, c_rows)
    kv[:RING] = near[...]
    kv[RING:] = far[...]
    total = softmax_passes(count, first, place, slots, bases, kv, q_t, probs, acc)
    inverse = 1.0 / total
    delta = jnp.sum(c_t[...].astype(jnp.float32) * acc[...], axis=0, keepdims=True) * inverse
    acc[...] = jnp.zeros_like(acc)
    dkv[...] = jnp.zeros_like(dkv)

    def grads(i, _):
        slot = slots[i]
        key_t = kv[slot, 0].T
        value = kv[slot, 1]
        dk = jnp.zeros((BLOCK, HD), jnp.float32)
        dv = jnp.zeros((BLOCK, HD), jnp.float32)
        for c in range(ROWS // WIDE):
            at = slice(c * WIDE, (c + 1) * WIDE)
            p = probs[i, :, at] * inverse[:, at]
            dp = dot(value, c_t[:, at])
            ds = (p * (dp - delta[:, at])).astype(jnp.bfloat16)
            dv += dot(p.astype(jnp.bfloat16), c_rows[at, :])
            dk += dot(ds, q_rows[at, :])
            acc[:, at] += dot(key_t, ds)
        dkv[slot, 0] = (dk * SCALE).astype(jnp.bfloat16)
        dkv[slot, 1] = dv.astype(jnp.bfloat16)
        return 0

    lax.fori_loop(0, count, grads, 0)
    for h in range(GROUP):
        at = slice(h * BLOCK, (h + 1) * BLOCK)
        dq[0, :, at] = (acc[:, at] * SCALE).T.astype(jnp.bfloat16)
    dnear[...] = dkv[:RING]
    dfar[...] = dkv[RING:]


SMEM = pl.BlockSpec(memory_space=pltpu.SMEM)
VMEM = pl.BlockSpec(memory_space=pltpu.VMEM)
HALF = jax.ShapeDtypeStruct((RING, 2, BLOCK, HD), jnp.bfloat16)
WHOLE = jax.ShapeDtypeStruct((1, BLOCK, GROUP * HD), jnp.bfloat16)
LIST = pltpu.SMEM((SLOTS + 1,), jnp.int32)
KV = pltpu.VMEM((SLOTS, 2, BLOCK, HD), jnp.bfloat16)
TALL = pltpu.VMEM((ROWS, HD), jnp.bfloat16)
FLAT = pltpu.VMEM((HD, ROWS), jnp.bfloat16)
PROBS = pltpu.VMEM((SLOTS, BLOCK, ROWS), jnp.float32)
ACC = pltpu.VMEM((HD, ROWS), jnp.float32)


def forward(order, lens, q, near, far):
    return pl.pallas_call(
        forward_kernel,
        out_shape=WHOLE,
        in_specs=[SMEM, SMEM, VMEM, VMEM, VMEM],
        out_specs=VMEM,
        scratch_shapes=[LIST, LIST, KV, FLAT, PROBS, ACC],
        compiler_params=pltpu.CompilerParams(vmem_limit_bytes=32 << 20),
        cost_estimate=pl.CostEstimate(flops=1 << 30, bytes_accessed=2 << 20, transcendentals=1 << 21),
        name="attend_forward",
    )(order, lens, q, near, far)


def backward(order, lens, q, cotan, near, far):
    return pl.pallas_call(
        backward_kernel,
        out_shape=(WHOLE, HALF, HALF),
        in_specs=[SMEM, SMEM, VMEM, VMEM, VMEM, VMEM],
        out_specs=(VMEM, VMEM, VMEM),
        scratch_shapes=[LIST, LIST, KV, FLAT, FLAT, TALL, TALL, PROBS, ACC, KV],
        compiler_params=pltpu.CompilerParams(vmem_limit_bytes=32 << 20),
        cost_estimate=pl.CostEstimate(flops=7 << 29, bytes_accessed=4 << 20, transcendentals=1 << 21),
        name="attend_backward",
    )(order, lens, q, cotan, near, far)


def along_z(x, distance):
    route = [(i, i // RING * RING + (i + distance) % RING) for i in range(SLOTS)]
    return lax.ppermute(x, "ctx", route)


def other_half(x):
    return lax.ppermute(x, "ctx", [(i, i ^ RING) for i in range(SLOTS)])


def other_section(x, flip):
    route = [(p * SLOTS + i, (1 - p) * SLOTS + (i ^ flip)) for p in range(2) for i in range(SLOTS)]
    return lax.ppermute(x, ("pipe", "ctx"), route)


def gather(block):
    x = block[None]
    below, above = along_z(x, 3), along_z(x, -3)
    lower = along_z(jnp.concatenate([x, below, above]), 1)
    upper = along_z(jnp.concatenate([x, below]), -1)
    near = jnp.concatenate([x, below, above, lower, upper])
    return near, other_half(near)


def add(*terms):
    total = terms[0].astype(jnp.float32)
    for term in terms[1:]:
        total = total + term.astype(jnp.float32)
    return total.astype(jnp.bfloat16)


def scatter(dnear, dfar):
    part = add(other_section(dnear, 0), other_section(dfar, RING))
    low = along_z(part[3:6], -1)
    high = along_z(part[6:8], 1)
    own = add(part[0], low[0], high[0])
    below = along_z(add(part[1], low[1], high[1]), -3)
    above = along_z(add(part[2], low[2]), 3)
    return add(own, below, above)


def shards(fwd_queries, fwd_keyvals, bwd_queries, bwd_keyvals, bwd_cotangent, doc_lengths, block_order):
    near, far = gather(bwd_keyvals[0])
    fnear, ffar = gather(fwd_keyvals[0])
    dq, dnear, dfar = backward(block_order, doc_lengths, bwd_queries, bwd_cotangent, near, far)
    keyval_grad = scatter(dnear, dfar)
    query_grad = lax.ppermute(dq, "pipe", [(0, 1), (1, 0)])
    output = forward(block_order, doc_lengths, fwd_queries, fnear, ffar)
    output = lax.ppermute(output, "pipe", [(0, 1), (1, 0)])
    return output, query_grad, keyval_grad[None]


def solution(mesh):
    placed = (
        P("pipe", "ctx", "tp"),
        P("pipe", None, "ctx", "tp"),
        P("pipe", "ctx", "tp"),
        P("pipe", None, "ctx", "tp"),
        P("pipe", "ctx", "tp"),
        P(),
        P(),
    )
    return jax.shard_map(
        shards,
        mesh=mesh,
        in_specs=placed,
        out_specs=(P("pipe", "ctx", "tp"), P("pipe", "ctx", "tp"), P("pipe", None, "ctx", "tp")),
        check_vma=False,
    )
```

time: 400 us -> 89.7 us (0.22)
  waiting for transfers between devices: 312 us -> 36.8 us
  starting transfers between devices: 2.91 us -> 39 us
  other arithmetic: 32.1 us -> 0.95 us
  matrix products: 29 us -> 0 us
  between operations: 14 us -> 0.84 us
  Pallas kernels: 0 us -> 9.83 us
  local copies, waits for them, and re-layouts: 8.81 us -> 2.5 us
    reduce_scatter x1 -> x0, waiting for transfers between devices: 181 us -> none  [shards(): lax.psum_scatter(keyval_grad.astype(jnp.bfloat16), 'ctx', scatter_dimensi...]
    all_gather x2 -> x0, waiting for transfers between devices: 127 us -> none  [the longest x1 72.5 us: shards(): lax.all_gather(bwd_keyvals[0], 'ctx', axis=1, tiled=True)]
    ppermute x3 -> x18, starting transfers between devices: 2.8 us -> 39 us  [the longest x12 29.5 us: along_z(): return lax.ppermute(x, 'ctx', route)]
    ppermute x3 -> x18, waiting for transfers between devices: 3.87 us -> 36.8 us  [the longest x12 18.8 us: along_z(): return lax.ppermute(x, 'ctx', route)]
    dot_general x8 -> x0, matrix products: 29 us -> none  [the longest x2 8.08 us: piece_scores(): jnp.einsum('qhgd,khd->hgqk', query, key, preferred_element_type=jnp.float32)]
    add x3 -> x0, other arithmetic: 20.1 us -> none  [the longest x2 20.1 us: layout(): position = starts + offsets]
    pallas_call x0 -> x2, Pallas kernels: none -> 9.83 us  [the longest x1 7.96 us: backward(): pl.pallas_call(backward_kernel, out_shape=(WHOLE, HALF, HALF), in_specs=[...]
    reduce_sum x4 -> x0, other arithmetic: 6.68 us -> none  [the longest x2 6.5 us: make_stats(): total = total * factor + jnp.sum(probs, axis=-1)]
  transfers between devices with their start and end apart: 6 -> 18, of which waited for: 4 -> 11; matrix products, arithmetic and copies ran while one was open for 12% -> 1% of each run, Pallas kernels for 0% -> 11%
where the time goes in v1:
time: 89.7 us; the launch traced here: 90 us
  starting transfers between devices  39 us (43%)
  waiting for transfers between devices  36.8 us (41%)
  Pallas kernels  9.83 us (11%)
  local copies, waits for them, and re-layouts  2.5 us (3%)
  other arithmetic  0.95 us (1%)
    ppermute x12, starting transfers between devices, along_z(): return lax.ppermute(x, 'ctx', route)  29.5 us
    ppermute x12, waiting for transfers between devices, along_z(): return lax.ppermute(x, 'ctx', route)  18.8 us
    ppermute x2, waiting for transfers between devices, other_section(): return lax.ppermute(x, ('pipe', 'ctx'), route)  18 us
    pallas_call x1, Pallas kernels, backward(): pl.pallas_call(backward_kernel, out_shape=(WHOLE, HALF, HALF), in_specs=[...  7.96 us
    ppermute x2, starting transfers between devices, other_half(): return lax.ppermute(x, 'ctx', [(i, i ^ RING) for i in range(SLOTS)])  6.7 us
    unnamed x24, local copies, waits for them, and re-layouts  2.44 us
    ppermute x1, starting transfers between devices, shards(): output = lax.ppermute(output, 'pipe', [(0, 1), (1, 0)])  1.9 us
    pallas_call x1, Pallas kernels, forward(): pl.pallas_call(forward_kernel, out_shape=WHOLE, in_specs=[SMEM, SMEM, VME...  1.88 us
  transfers between devices with their start and end apart: 18, of which 11 were waited for; matrix products, arithmetic and copies ran while one was open for 1% of the time, Pallas kernels for 11%

profile of v1, /device:TPU:8, one launch (start us, length us, event | category | flops | bytes accessed | tf_op | source)
XLA Modules:
  0.0 90.0 jit_solution(316277051180186615)
XLA Ops:
  0.6 4.7 %collective-permute-start.6 = (bf16[1,2,128,128]{3,2,1,0:T(8,128)(2,1)}, bf16[1,2,128,128]{3,2,1,0:T(8,128)(2,1)S(1)}, u32[]{:S(2)}, u32[]{:S(2)}) collective-permute-start(bf16[1,2,128,128]{3,2,1,0:T(8,128)(2,1)} %param.10), channel_id=1, source_target_pairs={{0,24},{8,32},{16,40},{24,48},{32,56},{40,0},{48,8},{56,16},{64,88... | collective-permute-start | bytes 196616 | tf_op jit(solution)/shard_map/ppermute | solution.py:185
  5.3 2.2 %collective-permute-start.7 = (bf16[1,2,128,128]{3,2,1,0:T(8,128)(2,1)}, bf16[1,2,128,128]{3,2,1,0:T(8,128)(2,1)S(1)}, u32[]{:S(2)}, u32[]{:S(2)}) collective-permute-start(bf16[1,2,128,128]{3,2,1,0:T(8,128)(2,1)} %param.10), channel_id=1, source_target_pairs={{0,40},{8,48},{16,56},{24,0},{32,8},{40,16},{48,24},{56,32},{64,10... | collective-permute-start | bytes 196616 | tf_op jit(solution)/shard_map/ppermute | solution.py:185
  7.6 0.9 constant_dynamic-update-slice_fusion.9
  8.4 1.5 %collective-permute-done.6 = bf16[1,2,128,128]{3,2,1,0:T(8,128)(2,1)S(1)} collective-permute-done((bf16[1,2,128,128]{3,2,1,0:T(8,128)(2,1)}, bf16[1,2,128,128]{3,2,1,0:T(8,128)(2,1)S(1)}, u32[]{:S(2)}, u32[]{:S(2)}) %collective-permute-start.6) | collective-permute-done | bytes 65568 | tf_op jit(solution)/shard_map/ppermute | solution.py:185
  10.0 2.0 %collective-permute-done.7 = bf16[1,2,128,128]{3,2,1,0:T(8,128)(2,1)S(1)} collective-permute-done((bf16[1,2,128,128]{3,2,1,0:T(8,128)(2,1)}, bf16[1,2,128,128]{3,2,1,0:T(8,128)(2,1)S(1)}, u32[]{:S(2)}, u32[]{:S(2)}) %collective-permute-start.7) | collective-permute-done | bytes 65568 | tf_op jit(solution)/shard_map/ppermute | solution.py:185
  12.0 5.4 %collective-permute-start.8 = (bf16[3,2,128,128]{3,2,1,0:T(8,128)(2,1)S(1)}, bf16[3,2,128,128]{3,2,1,0:T(8,128)(2,1)S(1)}, u32[]{:S(2)}, u32[]{:S(2)}) collective-permute-start(bf16[3,2,128,128]{3,2,1,0:T(8,128)(2,1)S(1)} %pad_maximum_fusion.1), channel_id=1, source_target_pairs={{0,8},{8,16},{16,24},{24,32},{32,40},{40,48},{48,56},{56,0},{64,72... | collective-permute-start | bytes 589832 | tf_op jit(solution)/shard_map/ppermute | solution.py:185
  17.4 0.1 collective-permute-start.9
  17.5 3.0 %collective-permute-done.8 = bf16[3,2,128,128]{3,2,1,0:T(8,128)(2,1)S(1)} collective-permute-done((bf16[3,2,128,128]{3,2,1,0:T(8,128)(2,1)S(1)}, bf16[3,2,128,128]{3,2,1,0:T(8,128)(2,1)S(1)}, u32[]{:S(2)}, u32[]{:S(2)}) %collective-permute-start.8) | collective-permute-done | bytes 196640 | tf_op jit(solution)/shard_map/ppermute | solution.py:185
  20.6 0.0 copy-start.6
  20.6 1.8 %collective-permute-done.9 = bf16[2,2,128,128]{3,2,1,0:T(8,128)(2,1)S(1)} collective-permute-done((bf16[2,2,128,128]{3,2,1,0:T(8,128)(2,1)S(1)}, bf16[2,2,128,128]{3,2,1,0:T(8,128)(2,1)S(1)}, u32[]{:S(2)}, u32[]{:S(2)}) %collective-permute-start.9) | collective-permute-done | bytes 131104 | tf_op jit(solution)/shard_map/ppermute | solution.py:185
  22.4 3.1 %collective-permute-start.10 = (bf16[8,2,128,128]{3,2,1,0:T(8,128)(2,1)S(1)}, bf16[8,2,128,128]{3,2,1,0:T(8,128)(2,1)S(1)}, u32[]{:S(2)}, u32[]{:S(2)}) collective-permute-start(bf16[8,2,128,128]{3,2,1,0:T(8,128)(2,1)S(1)} %constant_dynamic-update-slice_fusion.5.near), channel_id=1, source_target_pairs={{0,64},{8,72},{16,80},{24,88},{32,96},{40,104},{48,112},{56,120},{... | collective-permute-start | bytes 1572872 | tf_op jit(solution)/shard_map/ppermute | solution.py:189
  25.6 0.0 copy-done.6
  25.6 2.2 %collective-permute-start = (bf16[1,2,128,128]{3,2,1,0:T(8,128)(2,1)S(1)}, bf16[1,2,128,128]{3,2,1,0:T(8,128)(2,1)S(1)}, u32[]{:S(2)}, u32[]{:S(2)}) collective-permute-start(bf16[1,2,128,128]{3,2,1,0:T(8,128)(2,1)S(1)} %copy-done.6), channel_id=1, source_target_pairs={{0,24},{8,32},{16,40},{24,48},{32,56},{40,0},{48,8},{56,16},{64,88... | collective-permute-start | bytes 196616 | tf_op jit(solution)/shard_map/ppermute | solution.py:185
  27.8 2.8 %collective-permute-start.1 = (bf16[1,2,128,128]{3,2,1,0:T(8,128)(2,1)S(1)}, bf16[1,2,128,128]{3,2,1,0:T(8,128)(2,1)S(1)}, u32[]{:S(2)}, u32[]{:S(2)}) collective-permute-start(bf16[1,2,128,128]{3,2,1,0:T(8,128)(2,1)S(1)} %copy-done.6), channel_id=1, source_target_pairs={{0,40},{8,48},{16,56},{24,0},{32,8},{40,16},{48,24},{56,32},{64,10... | collective-permute-start | bytes 196616 | tf_op jit(solution)/shard_map/ppermute | solution.py:185
  30.6 2.5 %collective-permute-done = bf16[1,2,128,128]{3,2,1,0:T(8,128)(2,1)S(1)} collective-permute-done((bf16[1,2,128,128]{3,2,1,0:T(8,128)(2,1)S(1)}, bf16[1,2,128,128]{3,2,1,0:T(8,128)(2,1)S(1)}, u32[]{:S(2)}, u32[]{:S(2)}) %collective-permute-start) | collective-permute-done | bytes 65568 | tf_op jit(solution)/shard_map/ppermute | solution.py:185
  33.1 2.3 %collective-permute-done.1 = bf16[1,2,128,128]{3,2,1,0:T(8,128)(2,1)S(1)} collective-permute-done((bf16[1,2,128,128]{3,2,1,0:T(8,128)(2,1)S(1)}, bf16[1,2,128,128]{3,2,1,0:T(8,128)(2,1)S(1)}, u32[]{:S(2)}, u32[]{:S(2)}) %collective-permute-start.1) | collective-permute-done | bytes 65568 | tf_op jit(solution)/shard_map/ppermute | solution.py:185
  35.4 0.0 copy-start.3
  35.4 0.0 copy-start.4
  35.4 2.0 %collective-permute-start.2 = (bf16[3,2,128,128]{3,2,1,0:T(8,128)(2,1)S(1)}, bf16[3,2,128,128]{3,2,1,0:T(8,128)(2,1)S(1)}, u32[]{:S(2)}, u32[]{:S(2)}) collective-permute-start(bf16[3,2,128,128]{3,2,1,0:T(8,128)(2,1)S(1)} %pad_maximum_fusion), channel_id=1, source_target_pairs={{0,8},{8,16},{16,24},{24,32},{32,40},{40,48},{48,56},{56,0},{64,72... | collective-permute-start | bytes 589832 | tf_op jit(solution)/shard_map/ppermute | solution.py:185
  37.5 1.4 %collective-permute-start.3 = (bf16[2,2,128,128]{3,2,1,0:T(8,128)(2,1)S(1)}, bf16[2,2,128,128]{3,2,1,0:T(8,128)(2,1)S(1)}, u32[]{:S(2)}, u32[]{:S(2)}) collective-permute-start(bf16[2,2,128,128]{3,2,1,0:T(8,128)(2,1)S(1)} %pad_maximum_fusion.2), channel_id=1, source_target_pairs={{0,56},{8,0},{16,8},{24,16},{32,24},{40,32},{48,40},{56,48},{64,12... | collective-permute-start | bytes 393224 | tf_op jit(solution)/shard_map/ppermute | solution.py:185
  38.9 0.0 collective-permute-done.10.far
  38.9 8.0 %attend_backward.1 = (bf16[1,128,1024]{2,1,0:T(8,128)(2,1)S(1)}, bf16[8,2,128,128]{3,2,1,0:T(8,128)(2,1)S(1)}, bf16[8,2,128,128]{3,2,1,0:T(8,128)(2,1)S(1)}) custom-call(s32[2,16]{1,0:T(2,128)S(1)} %copy-done.3, s32[2,8]{1,0:T(2,128)S(1)} %copy-done.4, bf16[1,128,1024]{2,1,0:T(8,128)(2,1)S(1)} %copy-done, bf16[1,128,1024]{2,1,0:T(8,128)(2,1)S(1)} %copy-done.1, ...), custom_call_target="tpu_custom_call" | custom-call | flops 3758096384 | bytes 4194304 | tf_op jit(solution)/shard_map/attend_backward/pallas_call | solution.py:171
  46.9 0.7 collective-permute-start.12
  47.5 0.0 collective-permute-start.13
  47.6 0.0 collective-permute-done.2
  47.6 0.0 collective-permute-done.3
  47.7 3.6 %collective-permute-start.4 = (bf16[8,2,128,128]{3,2,1,0:T(8,128)(2,1)S(1)}, bf16[8,2,128,128]{3,2,1,0:T(8,128)(2,1)S(1)}, u32[]{:S(2)}, u32[]{:S(2)}) collective-permute-start(bf16[8,2,128,128]{3,2,1,0:T(8,128)(2,1)S(1)} %constant_dynamic-update-slice_fusion.near), channel_id=1, source_target_pairs={{0,64},{8,72},{16,80},{24,88},{32,96},{40,104},{48,112},{56,120},{... | collective-permute-start | bytes 1572872 | tf_op jit(solution)/shard_map/ppermute | solution.py:189
  51.2 10.6 %collective-permute-done.12 = bf16[8,2,128,128]{3,2,1,0:T(8,128)(2,1)S(1)} collective-permute-done((bf16[8,2,128,128]{3,2,1,0:T(8,128)(2,1)S(1)}, bf16[8,2,128,128]{3,2,1,0:T(8,128)(2,1)S(1)}, u32[]{:S(2)}, u32[]{:S(2)}) %collective-permute-start.12) | collective-permute-done | bytes 524320 | tf_op jit(solution)/shard_map/ppermute | solution.py:194
  61.8 7.4 %collective-permute-done.13 = bf16[8,2,128,128]{3,2,1,0:T(8,128)(2,1)S(1)} collective-permute-done((bf16[8,2,128,128]{3,2,1,0:T(8,128)(2,1)S(1)}, bf16[8,2,128,128]{3,2,1,0:T(8,128)(2,1)S(1)}, u32[]{:S(2)}, u32[]{:S(2)}) %collective-permute-start.13) | collective-permute-done | bytes 524320 | tf_op jit(solution)/shard_map/ppermute | solution.py:194
  69.2 0.1 add_convert_fusion
  69.4 0.0 copy-start.2
  69.4 0.1 collective-permute-start.14
  69.5 2.1 %collective-permute-start.15 = (bf16[2,2,128,128]{3,2,1,0:T(8,128)(2,1)S(1)}, bf16[2,2,128,128]{3,2,1,0:T(8,128)(2,1)S(1)}, u32[]{:S(2)}, u32[]{:S(2)}) collective-permute-start(bf16[2,2,128,128]{3,2,1,0:T(8,128)(2,1)S(1)} %slice.43), channel_id=1, source_target_pairs={{0,8},{8,16},{16,24},{24,32},{32,40},{40,48},{48,56},{56,0},{64,72... | collective-permute-start | bytes 393224 | tf_op jit(solution)/shard_map/ppermute | solution.py:185
  71.6 0.2 collective-permute-start.11
  71.8 0.0 collective-permute-done.4.far
  71.8 1.9 %attend_forward.1 = bf16[1,128,1024]{2,1,0:T(8,128)(2,1)S(1)} custom-call(s32[2,16]{1,0:T(2,128)S(1)} %copy-done.3, s32[2,8]{1,0:T(2,128)S(1)} %copy-done.4, bf16[1,128,1024]{2,1,0:T(8,128)(2,1)S(1)} %copy-done.2, bf16[8,2,128,128]{3,2,1,0:T(8,128)(2,1)S(1)} %constant_dynamic-update-slice_fusion.near, bf16[8,2,128,128]{3,2,1,0:T(8,128)(2,1)S(1)} %collective-permute-done.4.far), custom_call_target="tpu_custom_call" | custom-call | flops 1073741824 | bytes 2097152 | tf_op jit(solution)/shard_map/attend_forward/pallas_call | solution.py:158
  73.7 1.9 %collective-permute-start.5 = (bf16[1,128,1024]{2,1,0:T(8,128)(2,1)S(1)}, bf16[1,128,1024]{2,1,0:T(8,128)(2,1)S(1)}, u32[]{:S(2)}, u32[]{:S(2)}) collective-permute-start(bf16[1,128,1024]{2,1,0:T(8,128)(2,1)S(1)} %attend_forward.1), channel_id=1, source_target_pairs={{0,128},{128,0},{1,129},{129,1},{2,130},{130,2},{3,131},{131,3},{4... | collective-permute-start | bytes 786440 | tf_op jit(solution)/shard_map/ppermute | solution.py:230
  75.6 0.2 collective-permute-done.15
  75.8 0.0 collective-permute-done.14
  75.8 4.8 %collective-permute-start.16 = (bf16[2,128,128]{2,1,0:T(8,128)(2,1)S(1)}, bf16[2,128,128]{2,1,0:T(8,128)(2,1)S(1)}, u32[]{:S(2)}, u32[]{:S(2)}) collective-permute-start(bf16[2,128,128]{2,1,0:T(8,128)(2,1)S(1)} %get-tuple-element.9), channel_id=1, source_target_pairs={{0,40},{8,48},{16,56},{24,0},{32,8},{40,16},{48,24},{56,32},{64,10... | collective-permute-start | bytes 196616 | tf_op jit(solution)/shard_map/ppermute | solution.py:185
  80.6 1.7 %collective-permute-start.17 = (bf16[2,128,128]{2,1,0:T(8,128)(2,1)S(1)}, bf16[2,128,128]{2,1,0:T(8,128)(2,1)S(1)}, u32[]{:S(2)}, u32[]{:S(2)}) collective-permute-start(bf16[2,128,128]{2,1,0:T(8,128)(2,1)S(1)} %get-tuple-element.10), channel_id=1, source_target_pairs={{0,24},{8,32},{16,40},{24,48},{32,56},{40,0},{48,8},{56,16},{64,88... | collective-permute-start | bytes 196616 | tf_op jit(solution)/shard_map/ppermute | solution.py:185
  82.4 0.0 collective-permute-done.11
  82.4 0.0 collective-permute-done.5
  82.4 2.1 %collective-permute-done.16 = bf16[2,128,128]{2,1,0:T(8,128)(2,1)S(1)} collective-permute-done((bf16[2,128,128]{2,1,0:T(8,128)(2,1)S(1)}, bf16[2,128,128]{2,1,0:T(8,128)(2,1)S(1)}, u32[]{:S(2)}, u32[]{:S(2)}) %collective-permute-start.16) | collective-permute-done | bytes 65568 | tf_op jit(solution)/shard_map/ppermute | solution.py:185
  84.5 3.4 %collective-permute-done.17 = bf16[2,128,128]{2,1,0:T(8,128)(2,1)S(1)} collective-permute-done((bf16[2,128,128]{2,1,0:T(8,128)(2,1)S(1)}, bf16[2,128,128]{2,1,0:T(8,128)(2,1)S(1)}, u32[]{:S(2)}, u32[]{:S(2)}) %collective-permute-start.17) | collective-permute-done | bytes 65568 | tf_op jit(solution)/shard_map/ppermute | solution.py:185
  87.9 0.7 fusion.5
  88.6 0.7 copy.20
  89.3 0.7 copy.21
  (25 shorter events, 0.3 us)
Async XLA Ops:
  0.6 11.3 %copy-start.5 = (bf16[1,2,128,128]{3,2,1,0:T(8,128)(2,1)S(1)}, bf16[1,2,128,128]{3,2,1,0:T(8,128)(2,1)}, u32[]{:S(2)}) copy-start(bf16[1,2,128,128]{3,2,1,0:T(8,128)(2,1)} %param.10) | copy-start | bytes 196612
  0.6 9.3 %collective-permute-start.6 = (bf16[1,2,128,128]{3,2,1,0:T(8,128)(2,1)}, bf16[1,2,128,128]{3,2,1,0:T(8,128)(2,1)S(1)}, u32[]{:S(2)}, u32[]{:S(2)}) collective-permute-start(bf16[1,2,128,128]{3,2,1,0:T(8,128)(2,1)} %param.10), channel_id=1, source_target_pairs={{0,24},{8,32},{16,40},{24,48},{32,56},{40,0},{48,8},{56,16},{64,88... | collective-permute-start | bytes 196616 | tf_op jit(solution)/shard_map/ppermute | solution.py:185
  5.3 6.6 %collective-permute-start.7 = (bf16[1,2,128,128]{3,2,1,0:T(8,128)(2,1)}, bf16[1,2,128,128]{3,2,1,0:T(8,128)(2,1)S(1)}, u32[]{:S(2)}, u32[]{:S(2)}) collective-permute-start(bf16[1,2,128,128]{3,2,1,0:T(8,128)(2,1)} %param.10), channel_id=1, source_target_pairs={{0,40},{8,48},{16,56},{24,0},{32,8},{40,16},{48,24},{56,32},{64,10... | collective-permute-start | bytes 196616 | tf_op jit(solution)/shard_map/ppermute | solution.py:185
  12.0 8.6 %collective-permute-start.8 = (bf16[3,2,128,128]{3,2,1,0:T(8,128)(2,1)S(1)}, bf16[3,2,128,128]{3,2,1,0:T(8,128)(2,1)S(1)}, u32[]{:S(2)}, u32[]{:S(2)}) collective-permute-start(bf16[3,2,128,128]{3,2,1,0:T(8,128)(2,1)S(1)} %pad_maximum_fusion.1), channel_id=1, source_target_pairs={{0,8},{8,16},{16,24},{24,32},{32,40},{40,48},{48,56},{56,0},{64,72... | collective-permute-start | bytes 589832 | tf_op jit(solution)/shard_map/ppermute | solution.py:185
  17.4 5.0 %collective-permute-start.9 = (bf16[2,2,128,128]{3,2,1,0:T(8,128)(2,1)S(1)}, bf16[2,2,128,128]{3,2,1,0:T(8,128)(2,1)S(1)}, u32[]{:S(2)}, u32[]{:S(2)}) collective-permute-start(bf16[2,2,128,128]{3,2,1,0:T(8,128)(2,1)S(1)} %pad_maximum_fusion.3), channel_id=1, source_target_pairs={{0,56},{8,0},{16,8},{24,16},{32,24},{40,32},{48,40},{56,48},{64,12... | collective-permute-start | bytes 393224 | tf_op jit(solution)/shard_map/ppermute | solution.py:185
  20.6 5.0 %copy-start.6 = (bf16[1,2,128,128]{3,2,1,0:T(8,128)(2,1)S(1)}, bf16[1,2,128,128]{3,2,1,0:T(8,128)(2,1)}, u32[]{:S(2)}) copy-start(bf16[1,2,128,128]{3,2,1,0:T(8,128)(2,1)} %param.8) | copy-start | bytes 196612
  22.4 16.4 %collective-permute-start.10 = (bf16[8,2,128,128]{3,2,1,0:T(8,128)(2,1)S(1)}, bf16[8,2,128,128]{3,2,1,0:T(8,128)(2,1)S(1)}, u32[]{:S(2)}, u32[]{:S(2)}) collective-permute-start(bf16[8,2,128,128]{3,2,1,0:T(8,128)(2,1)S(1)} %constant_dynamic-update-slice_fusion.5.near), channel_id=1, source_target_pairs={{0,64},{8,72},{16,80},{24,88},{32,96},{40,104},{48,112},{56,120},{... | collective-permute-start | bytes 1572872 | tf_op jit(solution)/shard_map/ppermute | solution.py:189
  25.6 7.5 %collective-permute-start = (bf16[1,2,128,128]{3,2,1,0:T(8,128)(2,1)S(1)}, bf16[1,2,128,128]{3,2,1,0:T(8,128)(2,1)S(1)}, u32[]{:S(2)}, u32[]{:S(2)}) collective-permute-start(bf16[1,2,128,128]{3,2,1,0:T(8,128)(2,1)S(1)} %copy-done.6), channel_id=1, source_target_pairs={{0,24},{8,32},{16,40},{24,48},{32,56},{40,0},{48,8},{56,16},{64,88... | collective-permute-start | bytes 196616 | tf_op jit(solution)/shard_map/ppermute | solution.py:185
  27.8 7.6 %collective-permute-start.1 = (bf16[1,2,128,128]{3,2,1,0:T(8,128)(2,1)S(1)}, bf16[1,2,128,128]{3,2,1,0:T(8,128)(2,1)S(1)}, u32[]{:S(2)}, u32[]{:S(2)}) collective-permute-start(bf16[1,2,128,128]{3,2,1,0:T(8,128)(2,1)S(1)} %copy-done.6), channel_id=1, source_target_pairs={{0,40},{8,48},{16,56},{24,0},{32,8},{40,16},{48,24},{56,32},{64,10... | collective-permute-start | bytes 196616 | tf_op jit(solution)/shard_map/ppermute | solution.py:185
  30.6 8.3 %copy-start = (bf16[1,128,1024]{2,1,0:T(8,128)(2,1)S(1)}, bf16[1,128,1024]{2,1,0:T(8,128)(2,1)}, u32[]{:S(2)}) copy-start(bf16[1,128,1024]{2,1,0:T(8,128)(2,1)} %q.3) | copy-start | bytes 786436
  30.6 8.3 %copy-start.1 = (bf16[1,128,1024]{2,1,0:T(8,128)(2,1)S(1)}, bf16[1,128,1024]{2,1,0:T(8,128)(2,1)}, u32[]{:S(2)}) copy-start(bf16[1,128,1024]{2,1,0:T(8,128)(2,1)} %cotan.1) | copy-start | bytes 786436
  35.4 3.4 %copy-start.3 = (s32[2,16]{1,0:T(2,128)S(1)}, s32[2,16]{1,0:T(2,128)}, u32[]{:S(2)}) copy-start(s32[2,16]{1,0:T(2,128)} %order.3) | copy-start | bytes 388
  35.4 3.4 %copy-start.4 = (s32[2,8]{1,0:T(2,128)S(1)}, s32[2,8]{1,0:T(2,128)}, u32[]{:S(2)}) copy-start(s32[2,8]{1,0:T(2,128)} %lens.3) | copy-start | bytes 196
  35.4 12.1 %collective-permute-start.2 = (bf16[3,2,128,128]{3,2,1,0:T(8,128)(2,1)S(1)}, bf16[3,2,128,128]{3,2,1,0:T(8,128)(2,1)S(1)}, u32[]{:S(2)}, u32[]{:S(2)}) collective-permute-start(bf16[3,2,128,128]{3,2,1,0:T(8,128)(2,1)S(1)} %pad_maximum_fusion), channel_id=1, source_target_pairs={{0,8},{8,16},{16,24},{24,32},{32,40},{40,48},{48,56},{56,0},{64,72... | collective-permute-start | bytes 589832 | tf_op jit(solution)/shard_map/ppermute | solution.py:185
  37.5 10.1 %collective-permute-start.3 = (bf16[2,2,128,128]{3,2,1,0:T(8,128)(2,1)S(1)}, bf16[2,2,128,128]{3,2,1,0:T(8,128)(2,1)S(1)}, u32[]{:S(2)}, u32[]{:S(2)}) collective-permute-start(bf16[2,2,128,128]{3,2,1,0:T(8,128)(2,1)S(1)} %pad_maximum_fusion.2), channel_id=1, source_target_pairs={{0,56},{8,0},{16,8},{24,16},{32,24},{40,32},{48,40},{56,48},{64,12... | collective-permute-start | bytes 393224 | tf_op jit(solution)/shard_map/ppermute | solution.py:185
  46.9 14.9 %collective-permute-start.12 = (bf16[8,2,128,128]{3,2,1,0:T(8,128)(2,1)S(1)}, bf16[8,2,128,128]{3,2,1,0:T(8,128)(2,1)S(1)}, u32[]{:S(2)}, u32[]{:S(2)}) collective-permute-start(bf16[8,2,128,128]{3,2,1,0:T(8,128)(2,1)S(1)} %get-tuple-element.7), channel_id=1, source_target_pairs={{0,128},{8,136},{16,144},{24,152},{32,160},{40,168},{48,176},{56,1... | collective-permute-start | bytes 1572872 | tf_op jit(solution)/shard_map/ppermute | solution.py:194
  47.5 21.7 %collective-permute-start.13 = (bf16[8,2,128,128]{3,2,1,0:T(8,128)(2,1)S(1)}, bf16[8,2,128,128]{3,2,1,0:T(8,128)(2,1)S(1)}, u32[]{:S(2)}, u32[]{:S(2)}) collective-permute-start(bf16[8,2,128,128]{3,2,1,0:T(8,128)(2,1)S(1)} %get-tuple-element.8), channel_id=1, source_target_pairs={{0,192},{8,200},{16,208},{24,216},{32,224},{40,232},{48,240},{56,2... | collective-permute-start | bytes 1572872 | tf_op jit(solution)/shard_map/ppermute | solution.py:194
  47.7 24.2 %collective-permute-start.4 = (bf16[8,2,128,128]{3,2,1,0:T(8,128)(2,1)S(1)}, bf16[8,2,128,128]{3,2,1,0:T(8,128)(2,1)S(1)}, u32[]{:S(2)}, u32[]{:S(2)}) collective-permute-start(bf16[8,2,128,128]{3,2,1,0:T(8,128)(2,1)S(1)} %constant_dynamic-update-slice_fusion.near), channel_id=1, source_target_pairs={{0,64},{8,72},{16,80},{24,88},{32,96},{40,104},{48,112},{56,120},{... | collective-permute-start | bytes 1572872 | tf_op jit(solution)/shard_map/ppermute | solution.py:189
  69.4 2.5 %copy-start.2 = (bf16[1,128,1024]{2,1,0:T(8,128)(2,1)S(1)}, bf16[1,128,1024]{2,1,0:T(8,128)(2,1)}, u32[]{:S(2)}) copy-start(bf16[1,128,1024]{2,1,0:T(8,128)(2,1)} %q.2) | copy-start | bytes 786436
  69.4 6.4 %collective-permute-start.14 = (bf16[3,2,128,128]{3,2,1,0:T(8,128)(2,1)S(1)}, bf16[3,2,128,128]{3,2,1,0:T(8,128)(2,1)S(1)}, u32[]{:S(2)}, u32[]{:S(2)}) collective-permute-start(bf16[3,2,128,128]{3,2,1,0:T(8,128)(2,1)S(1)} %slice.41), channel_id=1, source_target_pairs={{0,56},{8,0},{16,8},{24,16},{32,24},{40,32},{48,40},{56,48},{64,12... | collective-permute-start | bytes 589832 | tf_op jit(solution)/shard_map/ppermute | solution.py:185
  69.5 6.3 %collective-permute-start.15 = (bf16[2,2,128,128]{3,2,1,0:T(8,128)(2,1)S(1)}, bf16[2,2,128,128]{3,2,1,0:T(8,128)(2,1)S(1)}, u32[]{:S(2)}, u32[]{:S(2)}) collective-permute-start(bf16[2,2,128,128]{3,2,1,0:T(8,128)(2,1)S(1)} %slice.43), channel_id=1, source_target_pairs={{0,8},{8,16},{16,24},{24,32},{32,40},{40,48},{48,56},{56,0},{64,72... | collective-permute-start | bytes 393224 | tf_op jit(solution)/shard_map/ppermute | solution.py:185
  71.6 10.8 %collective-permute-start.11 = (bf16[1,128,1024]{2,1,0:T(8,128)(2,1)S(1)}, bf16[1,128,1024]{2,1,0:T(8,128)(2,1)S(1)}, u32[]{:S(2)}, u32[]{:S(2)}) collective-permute-start(bf16[1,128,1024]{2,1,0:T(8,128)(2,1)S(1)} %get-tuple-element.6), channel_id=1, source_target_pairs={{0,128},{128,0},{1,129},{129,1},{2,130},{130,2},{3,131},{131,3},{4... | collective-permute-start | bytes 786440 | tf_op jit(solution)/shard_map/ppermute | solution.py:228
  73.7 8.7 %collective-permute-start.5 = (bf16[1,128,1024]{2,1,0:T(8,128)(2,1)S(1)}, bf16[1,128,1024]{2,1,0:T(8,128)(2,1)S(1)}, u32[]{:S(2)}, u32[]{:S(2)}) collective-permute-start(bf16[1,128,1024]{2,1,0:T(8,128)(2,1)S(1)} %attend_forward.1), channel_id=1, source_target_pairs={{0,128},{128,0},{1,129},{129,1},{2,130},{130,2},{3,131},{131,3},{4... | collective-permute-start | bytes 786440 | tf_op jit(solution)/shard_map/ppermute | solution.py:230
  75.8 8.7 %collective-permute-start.16 = (bf16[2,128,128]{2,1,0:T(8,128)(2,1)S(1)}, bf16[2,128,128]{2,1,0:T(8,128)(2,1)S(1)}, u32[]{:S(2)}, u32[]{:S(2)}) collective-permute-start(bf16[2,128,128]{2,1,0:T(8,128)(2,1)S(1)} %get-tuple-element.9), channel_id=1, source_target_pairs={{0,40},{8,48},{16,56},{24,0},{32,8},{40,16},{48,24},{56,32},{64,10... | collective-permute-start | bytes 196616 | tf_op jit(solution)/shard_map/ppermute | solution.py:185
  80.6 7.3 %collective-permute-start.17 = (bf16[2,128,128]{2,1,0:T(8,128)(2,1)S(1)}, bf16[2,128,128]{2,1,0:T(8,128)(2,1)S(1)}, u32[]{:S(2)}, u32[]{:S(2)}) collective-permute-start(bf16[2,128,128]{2,1,0:T(8,128)(2,1)S(1)} %get-tuple-element.10), channel_id=1, source_target_pairs={{0,24},{8,32},{16,40},{24,48},{32,56},{40,0},{48,8},{56,16},{64,88... | collective-permute-start | bytes 196616 | tf_op jit(solution)/shard_map/ppermute | solution.py:185

commit v2 on v0

v2 whole, which is shorter than its diff:
```python
import jax
import jax.numpy as jnp
from jax import lax
from jax.experimental import pallas as pl
from jax.experimental.pallas import tpu as pltpu
from jax.sharding import PartitionSpec as P

HD = 128
BLOCK = 128
GROUP = 8
ROWS = GROUP * BLOCK
WIDE = 2 * BLOCK
SLOTS = 16
PAIRS = 2 * 8 + 2
BEYOND = 1 << 20
EXTRA = 16
PACK = 12
ADD = 12
GRADS = 40
TURN = 12
FORWARD = 12
FINISH = 4
RING = 8
OFFSETS = (0, -3, 3, -1, -4, 2, 1, -2)
SCALE = HD**-0.5
LOG2E = 1.4426950408889634
NEG = -1e30


def prepare(batch, table, slots, sides, bases, first, place):
    me = lax.axis_index("ctx")
    half, z = me // RING, me % RING
    query_bases, leasts = [], []
    for side in range(2):
        owner = (half + side) % 2 * RING + z
        query_base = table[batch, owner] * BLOCK
        at = query_base + lax.broadcasted_iota(jnp.int32, (8, BLOCK), 1)
        start = jnp.zeros((8, BLOCK), jnp.int32)
        least = jnp.int32(0)
        end = jnp.int32(0)
        for i in range(SLOTS, table.shape[1]):
            end = end + table[batch, i]
            start = jnp.where(at >= end, end, start)
            least = jnp.where(query_base >= end, end, least)
        first[side] = start
        place[side] = at
        query_bases.append(query_base)
        leasts.append(least)
    count = jnp.int32(0)
    for side in range(2):
        for slot in range(RING):
            owner = half * RING + (z + (OFFSETS[slot] + RING)) % RING
            base = table[batch, owner] * BLOCK
            slots[count] = slot
            sides[count] = side
            bases[count] = base
            active = (base <= query_bases[side]) & (base + (BLOCK - 1) >= leasts[side])
            count = count + active.astype(jnp.int32)
        slots[count] = 0
        bases[count] = BEYOND
        count = count + count % 2
    return count // 2


def dot(a, b):
    return jnp.dot(a, b, preferred_element_type=jnp.float32)


def add(*terms):
    total = terms[0].astype(jnp.float32)
    for term in terms[1:]:
        total = total + term.astype(jnp.float32)
    return total.astype(jnp.bfloat16)


def turn(ref, flat, tall=None):
    for h in range(GROUP):
        part = ref[0, :, h * HD : (h + 1) * HD]
        flat[:, h * BLOCK : (h + 1) * BLOCK] = part.T
        if tall is not None:
            tall[h * BLOCK : (h + 1) * BLOCK, :] = part


def total_kernel(own, below, above, _, out):
    out[0] = add(own[...], below[...], above[...])


def turn_kernel(q, c, q_far, c_far, _, q_t, c_t, q_rows, c_rows):
    turn(q, q_t.at[0], q_rows.at[0])
    turn(c, c_t.at[0], c_rows.at[0])
    turn(q_far, q_t.at[1], q_rows.at[1])
    turn(c_far, c_t.at[1], c_rows.at[1])


def allowed(i, side, bases, first, place):
    row = bases[i] + lax.broadcasted_iota(jnp.int32, (BLOCK, BLOCK), 0)
    return (row >= first[side, 0:1]) & (row <= place[side, 0:1])


def masked_scores(key, q_t, side, mask, c):
    s = dot(key, q_t[side, :, c * WIDE : (c + 1) * WIDE])
    return [
        jnp.where(mask, s[:, j * BLOCK : (j + 1) * BLOCK], NEG) for j in range(WIDE // BLOCK)
    ]


def fold(x, op):
    return op(x.reshape(x.shape[0] // 8, 8, x.shape[1]), axis=0)


def largest(count, slots, sides, bases, first, place, kv, q_t, scores, tops):
    def body(g, _):
        side = sides[2 * g]
        keys = [kv[slots[2 * g + j], 0] for j in range(2)]
        masks = [allowed(2 * g + j, side, bases, first, place) for j in range(2)]
        for c in range(ROWS // WIDE):
            for j in range(2):
                for k, part in enumerate(masked_scores(keys[j], q_t, side, masks[j], c)):
                    at = slice(c * WIDE + k * BLOCK, c * WIDE + (k + 1) * BLOCK)
                    scores[2 * g + j, :, at] = part
                    tops[side, :, at] = jnp.maximum(tops[side, :, at], fold(part, jnp.max))
        return 0

    lax.fori_loop(0, count, body, 0)
    for side in range(2):
        tops[side] = jnp.broadcast_to(jnp.max(tops[side], axis=0, keepdims=True), (8, ROWS))


def statistics(count, slots, sides, bases, first, place, kv, q_t, c_t, scores, tops, totals, deltas):
    tops[...] = jnp.full(tops.shape, NEG, jnp.float32)
    totals[...] = jnp.zeros(totals.shape, jnp.float32)
    deltas[...] = jnp.zeros(deltas.shape, jnp.float32)

    largest(count, slots, sides, bases, first, place, kv, q_t, scores, tops)

    def sums(g, _):
        side = sides[2 * g]
        values = [kv[slots[2 * g + j], 1] for j in range(2)]
        for c in range(ROWS // WIDE):
            at = slice(c * WIDE, (c + 1) * WIDE)
            for j in range(2):
                p = jnp.exp2((scores[2 * g + j, :, at] - tops[side, 0:1, at]) * (SCALE * LOG2E))
                totals[side, :, at] += fold(p, jnp.sum)
                deltas[side, :, at] += fold(p * dot(values[j], c_t[side, :, at]), jnp.sum)
        return 0

    lax.fori_loop(0, count, sums, 0)
    rows = []
    for side in range(2):
        rows.append(tops[side, 0:1])
        rows.append(jnp.sum(totals[side], axis=0, keepdims=True))
        rows.append(jnp.sum(deltas[side], axis=0, keepdims=True))
    rows.append(jnp.zeros((8 - len(rows), ROWS), jnp.float32))
    return jnp.concatenate(rows, axis=0)


def merge(mine, other, per_side=3):
    merged = []
    for side in range(2):
        a = [mine[side * per_side + r : side * per_side + r + 1, :] for r in range(per_side)]
        b = [other[(1 - side) * per_side + r : (1 - side) * per_side + r + 1, :] for r in range(per_side)]
        top = jnp.maximum(a[0], b[0])
        fa = jnp.exp2((a[0] - top) * (SCALE * LOG2E))
        fb = jnp.exp2((b[0] - top) * (SCALE * LOG2E))
        merged.append([top] + [x * fa + y * fb for x, y in zip(a[1:], b[1:])])
    return merged


def backward_stats_kernel(
    table, q_t, c_t, near, out,
    slots, sides, bases, first, place, scores, tops, totals, deltas,
):
    near = near.at[0]
    count = prepare(0, table, slots, sides, bases, first, place)
    out[...] = statistics(
        count, slots, sides, bases, first, place, near, q_t, c_t, scores, tops, totals, deltas
    )


def thirds(x):
    parts = []
    for _ in range(3):
        part = x.astype(jnp.bfloat16).astype(jnp.float32)
        parts.append(part)
        x = x - part
    return parts


def forward_kernel(
    table, q, q_far, near, _, out, out_far,
    slots, sides, bases, first, place, q_t, scores, tops, totals, acc, turned, probs,
):
    near = near.at[1]
    count = prepare(1, table, slots, sides, bases, first, place)
    turn(q, q_t.at[0])
    turn(q_far, q_t.at[1])
    tops[...] = jnp.full(tops.shape, NEG, jnp.float32)
    totals[...] = jnp.zeros(totals.shape, jnp.float32)
    acc[...] = jnp.zeros_like(acc)
    largest(count, slots, sides, bases, first, place, near, q_t, scores, tops)

    def body(g, _):
        side = sides[2 * g]
        for j in range(2):
            turned[:, j * BLOCK : (j + 1) * BLOCK] = near[slots[2 * g + j], 1].T
        for c in range(ROWS // WIDE):
            at = slice(c * WIDE, (c + 1) * WIDE)
            for j in range(2):
                p = jnp.exp2((scores[2 * g + j, :, at] - tops[side, 0:1, at]) * (SCALE * LOG2E))
                totals[side, :, at] += fold(p, jnp.sum)
                probs[j * BLOCK : (j + 1) * BLOCK, at] = p.astype(jnp.bfloat16)
        acc[side] += dot(turned[...], probs[...])
        return 0

    lax.fori_loop(0, count, body, 0)
    for side, ref in enumerate((out, out_far)):
        total = jnp.sum(totals[side], axis=0, keepdims=True)
        total = jnp.maximum(total, 1e-30)
        inverse = 1.0 / total
        for h in range(GROUP):
            at = slice(h * BLOCK, (h + 1) * BLOCK)
            ref[0, :BLOCK, at] = (acc[side, :, at] * inverse[:, at]).T.astype(jnp.bfloat16)
        logs = tops[side, 0:1] * (SCALE * LOG2E) + jnp.log2(total)
        pad = jnp.zeros((EXTRA - 3, ROWS), jnp.float32)
        ref[0, BLOCK:] = jnp.concatenate(thirds(logs) + [pad], axis=0).astype(jnp.bfloat16)


def add_kernel(keep, low, high, _a, _b, own, below, above):
    own[...] = add(keep[0], low[0], high[0])
    below[...] = add(keep[1], low[1], high[1])
    above[...] = add(keep[2], low[2])


def pack_kernel(x, below, above, three, two):
    for i, ref in enumerate((x, below, above)):
        three[:, i : i + 1] = ref[...]
        if i < 2:
            two[:, i : i + 1] = ref[...]


def finish_kernel(dq, dq_far, a, b, query_grad, output, token):
    token[...] = jnp.zeros(token.shape, token.dtype)
    query_grad[...] = add(dq[...], dq_far[...])
    logs = []
    for ref in (a, b):
        rows = ref[0, BLOCK:].astype(jnp.float32)
        logs.append(rows[0:1] + rows[1:2] + rows[2:3])
    top = jnp.maximum(logs[0], logs[1])
    wa, wb = jnp.exp2(logs[0] - top), jnp.exp2(logs[1] - top)
    inverse = 1.0 / (wa + wb)
    wa, wb = wa * inverse, wb * inverse
    for h in range(GROUP):
        at = slice(h * BLOCK, (h + 1) * BLOCK)
        one = jnp.broadcast_to(wa[:, at], (BLOCK, BLOCK)).T
        two = jnp.broadcast_to(wb[:, at], (BLOCK, BLOCK)).T
        x, y = a[0, :BLOCK, at].astype(jnp.float32), b[0, :BLOCK, at].astype(jnp.float32)
        output[0, :, at] = (x * one + y * two).astype(jnp.bfloat16)


def backward_kernel(
    table, q_t, c_t, q_rows, c_rows, near, mine, other, _, dq, dq_far, keep, low, high,
    slots, sides, bases, first, place, rows, acc, dkv, turned, probs, dscores,
):
    near = near.at[0]
    count = prepare(0, table, slots, sides, bases, first, place)
    for side, (top, total, weighted) in enumerate(merge(mine, other)):
        rows[side, 0:1] = top * (SCALE * LOG2E) + jnp.log2(total)
        rows[side, 1:2] = weighted / total
    acc[...] = jnp.zeros_like(acc)
    dkv[...] = jnp.zeros_like(dkv)

    def grads(g, _):
        side = sides[2 * g]
        for j in range(2):
            at_rows = slice(j * BLOCK, (j + 1) * BLOCK)
            key = near[slots[2 * g + j], 0]
            value = near[slots[2 * g + j], 1]
            mask = allowed(2 * g + j, side, bases, first, place)
            turned[:, at_rows] = key.T
            for c in range(ROWS // WIDE):
                at = slice(c * WIDE, (c + 1) * WIDE)
                s = jnp.concatenate(masked_scores(key, q_t, side, mask, c), axis=1)
                p = jnp.exp2(s * (SCALE * LOG2E) - rows[side, 0:1, at])
                dp = dot(value, c_t[side, :, at])
                probs[at_rows, at] = p.astype(jnp.bfloat16)
                dscores[at_rows, at] = (p * (dp - rows[side, 1:2, at])).astype(jnp.bfloat16)
        dv = dot(probs[...], c_rows[side])
        dk = dot(dscores[...], q_rows[side]) * SCALE
        acc[side] += dot(turned[...], dscores[...])
        for j in range(2):
            at_rows = slice(j * BLOCK, (j + 1) * BLOCK)
            dkv[slots[2 * g + j], 0] += dk[at_rows]
            dkv[slots[2 * g + j], 1] += dv[at_rows]
        return 0

    lax.fori_loop(0, count, grads, 0)
    keep[...] = dkv[0:3].astype(jnp.bfloat16)
    low[...] = dkv[3:6].astype(jnp.bfloat16)
    high[...] = dkv[6:8].astype(jnp.bfloat16)
    for side, ref in enumerate((dq, dq_far)):
        for h in range(GROUP):
            at = slice(h * BLOCK, (h + 1) * BLOCK)
            ref[0, :, at] = (acc[side, :, at] * SCALE).T.astype(jnp.bfloat16)


SMEM = pl.BlockSpec(memory_space=pltpu.SMEM)
VMEM = pl.BlockSpec(memory_space=pltpu.VMEM)
WHOLE = jax.ShapeDtypeStruct((1, BLOCK, GROUP * HD), jnp.bfloat16)
TOKEN = jax.ShapeDtypeStruct((8, 128), jnp.float32)
STATS = jax.ShapeDtypeStruct((8, ROWS), jnp.float32)
LIST = pltpu.SMEM((PAIRS + 1,), jnp.int32)
PLACES = pltpu.VMEM((2, 8, BLOCK), jnp.int32)
LISTS = [LIST, LIST, LIST, PLACES, PLACES]
TALLS = jax.ShapeDtypeStruct((2, ROWS, HD), jnp.bfloat16)
FLATS = jax.ShapeDtypeStruct((2, HD, ROWS), jnp.bfloat16)
FLAT = pltpu.VMEM((2, HD, ROWS), jnp.bfloat16)
PART = jax.ShapeDtypeStruct((2, BLOCK, HD), jnp.bfloat16)
TALLER = jax.ShapeDtypeStruct((1, BLOCK + EXTRA, GROUP * HD), jnp.bfloat16)
SCORES = pltpu.VMEM((PAIRS, BLOCK, ROWS), jnp.float32)
ACC = pltpu.VMEM((2, HD, ROWS), jnp.float32)
TURNED = pltpu.VMEM((HD, 2 * BLOCK), jnp.bfloat16)
PROBS = pltpu.VMEM((2 * BLOCK, ROWS), jnp.bfloat16)
SUMS = pltpu.VMEM((2, 8, ROWS), jnp.float32)
DKV = pltpu.VMEM((RING, 2, BLOCK, HD), jnp.float32)


def blocks(n):
    return jax.ShapeDtypeStruct((n, 2, BLOCK, HD), jnp.bfloat16)


def pairs(n):
    return jax.ShapeDtypeStruct((2, n, 2, BLOCK, HD), jnp.bfloat16)


def kernel(body, name, outs, scratch, cost, args, lists=()):
    single = not isinstance(outs, tuple)
    return pl.pallas_call(
        body,
        out_shape=outs,
        in_specs=[SMEM] * len(lists) + [VMEM] * len(args),
        out_specs=VMEM if single else (VMEM,) * len(outs),
        scratch_shapes=(LISTS if lists else []) + scratch,
        compiler_params=pltpu.CompilerParams(vmem_limit_bytes=32 << 20),
        cost_estimate=pl.CostEstimate(
            flops=cost << 29, bytes_accessed=2 << 20, transcendentals=1 << 21
        ),
        name=name,
    )(*lists, *args)


def along_z(x, distance):
    route = [(i, i // RING * RING + (i + distance) % RING) for i in range(SLOTS)]
    return lax.ppermute(x, "ctx", route)


def across_x(x):
    return lax.ppermute(x, "ctx", [(i, i ^ RING) for i in range(SLOTS)])


def other_section(x, flip=0, distance=0):
    route = [
        (p * SLOTS + i, (1 - p) * SLOTS + (i // RING * RING + (i + distance) % RING ^ flip))
        for p in range(2)
        for i in range(SLOTS)
    ]
    return lax.ppermute(x, ("pipe", "ctx"), route)


def gather(x):
    below, above = along_z(x, 3), along_z(x, -3)
    three, two = kernel(pack_kernel, "pack", (pairs(3), pairs(2)), [], PACK, (x, below, above))
    return jnp.concatenate([three, along_z(three, 1), along_z(two, -1)], axis=1), three


def shards(fwd_queries, fwd_keyvals, bwd_queries, bwd_keyvals, bwd_cotangent, doc_lengths, block_order):
    lists = (jnp.concatenate([block_order, doc_lengths], axis=1),)
    near, three = gather(jnp.stack([bwd_keyvals, fwd_keyvals]))
    q_t, c_t, q_rows, c_rows = kernel(
        turn_kernel, "turn", (FLATS, FLATS, TALLS, TALLS), [], TURN,
        (bwd_queries, bwd_cotangent, across_x(bwd_queries), across_x(bwd_cotangent), three),
    )
    mine = kernel(
        backward_stats_kernel, "backward_stats", STATS,
        [SCORES, SUMS, SUMS, SUMS], 2, (q_t, c_t, near), lists,
    )
    other = across_x(mine)
    out, out_far = kernel(
        forward_kernel, "forward", (TALLER, TALLER),
        [FLAT, SCORES, SUMS, SUMS, ACC, TURNED, PROBS], FORWARD, (fwd_queries, across_x(fwd_queries), near, mine), lists,
    )
    dq, dq_far, keep, low, high = kernel(
        backward_kernel, "backward_grads", (WHOLE, WHOLE, blocks(3), blocks(3), blocks(2)),
        [SUMS, ACC, DKV, TURNED, PROBS, PROBS], GRADS, (q_t, c_t, q_rows, c_rows, near, mine, other, out), lists,
    )
    out, out_far = other_section(out), other_section(out_far, RING)
    low, high = along_z(low, -1), along_z(high, 1)
    dq, dq_far = other_section(dq), other_section(dq_far, RING)
    own, below, above = kernel(
        add_kernel, "add", (PART, PART, PART), [], ADD, (keep, low, high, out, out_far),
    )
    own, below, above = other_section(own), other_section(below, 0, -3), other_section(above, 0, 3)
    query_grad, output, token = kernel(
        finish_kernel, "finish", (WHOLE, WHOLE, TOKEN), [], FINISH, (dq, dq_far, out, out_far)
    )
    keyval_grad = kernel(total_kernel, "total", blocks(1), [], 0, (own, below, above, token))
    return output, query_grad, keyval_grad


def solution(mesh):
    placed = (
        P("pipe", "ctx", "tp"),
        P("pipe", None, "ctx", "tp"),
        P("pipe", "ctx", "tp"),
        P("pipe", None, "ctx", "tp"),
        P("pipe", "ctx", "tp"),
        P(),
        P(),
    )
    return jax.shard_map(
        shards,
        mesh=mesh,
        in_specs=placed,
        out_specs=(P("pipe", "ctx", "tp"), P("pipe", "ctx", "tp"), P("pipe", None, "ctx", "tp")),
        check_vma=False,
    )
```

time: 400 us -> 67.5 us (0.17)
  waiting for transfers between devices: 312 us -> 23.6 us
  other arithmetic: 32.1 us -> 1 us
  matrix products: 29 us -> 0 us
  starting transfers between devices: 2.91 us -> 31.7 us
  between operations: 14 us -> 0.77 us
  Pallas kernels: 0 us -> 9.85 us
  local copies, waits for them, and re-layouts: 8.81 us -> 0.14 us
    reduce_scatter x1 -> x0, waiting for transfers between devices: 181 us -> none  [shards(): lax.psum_scatter(keyval_grad.astype(jnp.bfloat16), 'ctx', scatter_dimensi...]
    all_gather x2 -> x0, waiting for transfers between devices: 127 us -> none  [the longest x1 72.5 us: shards(): lax.all_gather(bwd_keyvals[0], 'ctx', axis=1, tiled=True)]
    dot_general x8 -> x0, matrix products: 29 us -> none  [the longest x2 8.08 us: piece_scores(): jnp.einsum('qhgd,khd->hgqk', query, key, preferred_element_type=jnp.float32)]
    ppermute x3 -> x17, starting transfers between devices: 2.8 us -> 31.7 us  [the longest x6 11 us: along_z(): return lax.ppermute(x, 'ctx', route)]
    add x3 -> x0, other arithmetic: 20.1 us -> none  [the longest x2 20.1 us: layout(): position = starts + offsets]
    ppermute x3 -> x17, waiting for transfers between devices: 3.87 us -> 23.6 us  [the longest x6 14.2 us: along_z(): return lax.ppermute(x, 'ctx', route)]
    pallas_call x0 -> x8, Pallas kernels: none -> 9.85 us  [kernel(): pl.pallas_call(body, out_shape=outs, in_specs=[SMEM] * len(lists) + [VMEM...]
    reduce_sum x4 -> x0, other arithmetic: 6.68 us -> none  [the longest x2 6.5 us: make_stats(): total = total * factor + jnp.sum(probs, axis=-1)]
  transfers between devices with their start and end apart: 6 -> 17, of which waited for: 4 -> 8; matrix products, arithmetic and copies ran while one was open for 12% -> 0% of each run, Pallas kernels for 0% -> 14%
where the time goes in v2:
time: 67.5 us; the launch traced here: 67 us
  starting transfers between devices  31.7 us (47%)
  waiting for transfers between devices  23.6 us (35%)
  Pallas kernels  9.85 us (15%)
  other arithmetic  1 us (1%)
  between operations  0.77 us (1%)
    ppermute x6, waiting for transfers between devices, along_z(): return lax.ppermute(x, 'ctx', route)  14.2 us
    ppermute x6, starting transfers between devices, along_z(): return lax.ppermute(x, 'ctx', route)  11 us
    ppermute x7, starting transfers between devices, other_section(): return lax.ppermute(x, ('pipe', 'ctx'), route)  10.4 us
    ppermute x4, starting transfers between devices, across_x(): return lax.ppermute(x, 'ctx', [(i, i ^ RING) for i in range(SLOTS)])  10.3 us
    pallas_call x8, Pallas kernels, kernel(): pl.pallas_call(body, out_shape=outs, in_specs=[SMEM] * len(lists) + [VMEM...  9.85 us
    ppermute x4, waiting for transfers between devices, across_x(): return lax.ppermute(x, 'ctx', [(i, i ^ RING) for i in range(SLOTS)])  5.6 us
    ppermute x7, waiting for transfers between devices, other_section(): return lax.ppermute(x, ('pipe', 'ctx'), route)  3.78 us
  transfers between devices with their start and end apart: 17, of which 8 were waited for; matrix products, arithmetic and copies ran while one was open for 0% of the time, Pallas kernels for 14%

profile of v2, /device:TPU:8, one launch (start us, length us, event | category | flops | bytes accessed | tf_op | source)
XLA Modules:
  0.0 67.0 jit_solution(5446507811640455552)
XLA Ops:
  0.7 0.9 %pad_maximum_fusion.x = bf16[2,1,2,128,128]{4,3,2,1,0:T(8,128)(2,1)S(1)} fusion(bf16[1,1,2,128,128]{4,3,2,1,0:T(8,128)(2,1)} %bitcast.2, bf16[1,1,2,128,128]{4,3,2,1,0:T(8,128)(2,1)} %bitcast.3), kind=kLoop, calls=%fused_computation | loop fusion | flops 65536 | bytes 262144 | tf_op jit(solution)/shard_map/stack | solution.py:377
  1.6 6.8 %collective-permute-start.3 = (bf16[2,1,2,128,128]{4,3,2,1,0:T(8,128)(2,1)S(1)}, bf16[2,1,2,128,128]{4,3,2,1,0:T(8,128)(2,1)S(1)}, u32[]{:S(2)}, u32[]{:S(2)}) collective-permute-start(bf16[2,1,2,128,128]{4,3,2,1,0:T(8,128)(2,1)S(1)} %pad_maximum_fusion.x), channel_id=1, source_target_pairs={{0,40},{8,48},{16,56},{24,0},{32,8},{40,16},{48,24},{56,32},{64,10... | collective-permute-start | bytes 393224 | tf_op jit(solution)/shard_map/ppermute | solution.py:353
  8.4 0.0 collective-permute-start.2
  8.4 3.0 %collective-permute-start.7 = (bf16[1,128,1024]{2,1,0:T(8,128)(2,1)}, bf16[1,128,1024]{2,1,0:T(8,128)(2,1)S(1)}, u32[]{:S(2)}, u32[]{:S(2)}) collective-permute-start(bf16[1,128,1024]{2,1,0:T(8,128)(2,1)} %q.3), channel_id=1, source_target_pairs={{0,64},{8,72},{16,80},{24,88},{32,96},{40,104},{48,112},{56,120},{... | collective-permute-start | bytes 786440 | tf_op jit(solution)/shard_map/ppermute | solution.py:357
  11.4 0.5 collective-permute-start
  11.9 3.0 %collective-permute-start.1 = (bf16[1,128,1024]{2,1,0:T(8,128)(2,1)}, bf16[1,128,1024]{2,1,0:T(8,128)(2,1)S(1)}, u32[]{:S(2)}, u32[]{:S(2)}) collective-permute-start(bf16[1,128,1024]{2,1,0:T(8,128)(2,1)} %c.1), channel_id=1, source_target_pairs={{0,64},{8,72},{16,80},{24,88},{32,96},{40,104},{48,112},{56,120},{... | collective-permute-start | bytes 786440 | tf_op jit(solution)/shard_map/ppermute | solution.py:357
  15.0 0.1 pad_add_fusion.table
  15.1 1.7 %collective-permute-done.3.above = bf16[2,1,2,128,128]{4,3,2,1,0:T(8,128)(2,1)S(1)} collective-permute-done((bf16[2,1,2,128,128]{4,3,2,1,0:T(8,128)(2,1)S(1)}, bf16[2,1,2,128,128]{4,3,2,1,0:T(8,128)(2,1)S(1)}, u32[]{:S(2)}, u32[]{:S(2)}) %collective-permute-start.3) | collective-permute-done | bytes 131104 | tf_op jit(solution)/shard_map/ppermute | solution.py:353
  16.8 4.5 %collective-permute-done.2.below = bf16[2,1,2,128,128]{4,3,2,1,0:T(8,128)(2,1)S(1)} collective-permute-done((bf16[2,1,2,128,128]{4,3,2,1,0:T(8,128)(2,1)S(1)}, bf16[2,1,2,128,128]{4,3,2,1,0:T(8,128)(2,1)S(1)}, u32[]{:S(2)}, u32[]{:S(2)}) %collective-permute-start.2) | collective-permute-done | bytes 131104 | tf_op jit(solution)/shard_map/ppermute | solution.py:353
  21.3 0.1 pack.1
  21.4 0.1 collective-permute-start.5
  21.5 0.0 copy-start.1
  21.5 2.0 %collective-permute-start.4 = (bf16[2,3,2,128,128]{4,3,2,1,0:T(8,128)(2,1)S(1)}, bf16[2,3,2,128,128]{4,3,2,1,0:T(8,128)(2,1)S(1)}, u32[]{:S(2)}, u32[]{:S(2)}) collective-permute-start(bf16[2,3,2,128,128]{4,3,2,1,0:T(8,128)(2,1)S(1)} %get-tuple-element.22._), channel_id=1, source_target_pairs={{0,8},{8,16},{16,24},{24,32},{32,40},{40,48},{48,56},{56,0},{64,72... | collective-permute-start | bytes 1179656 | tf_op jit(solution)/shard_map/ppermute | solution.py:353
  23.5 1.4 %collective-permute-done.q_far = bf16[1,128,1024]{2,1,0:T(8,128)(2,1)S(1)} collective-permute-done((bf16[1,128,1024]{2,1,0:T(8,128)(2,1)S(1)}, bf16[1,128,1024]{2,1,0:T(8,128)(2,1)S(1)}, u32[]{:S(2)}, u32[]{:S(2)}) %collective-permute-start) | collective-permute-done | bytes 262176 | tf_op jit(solution)/shard_map/ppermute | solution.py:357
  25.0 4.2 %collective-permute-done.1.c_far = bf16[1,128,1024]{2,1,0:T(8,128)(2,1)S(1)} collective-permute-done((bf16[1,128,1024]{2,1,0:T(8,128)(2,1)}, bf16[1,128,1024]{2,1,0:T(8,128)(2,1)S(1)}, u32[]{:S(2)}, u32[]{:S(2)}) %collective-permute-start.1) | collective-permute-done | bytes 262176 | tf_op jit(solution)/shard_map/ppermute | solution.py:357
  29.1 0.0 copy-done.1
  29.1 0.4 turn.1
  29.5 3.8 %collective-permute-done.4 = bf16[2,3,2,128,128]{4,3,2,1,0:T(8,128)(2,1)S(1)} collective-permute-done((bf16[2,3,2,128,128]{4,3,2,1,0:T(8,128)(2,1)S(1)}, bf16[2,3,2,128,128]{4,3,2,1,0:T(8,128)(2,1)S(1)}, u32[]{:S(2)}, u32[]{:S(2)}) %collective-permute-start.4) | collective-permute-done | bytes 393248 | tf_op jit(solution)/shard_map/ppermute | solution.py:353
  33.3 0.1 constant_dynamic-update-slice_fusion.1
  33.4 0.0 collective-permute-done.5
  33.4 0.0 copy-start.2
  33.4 2.0 %backward_stats.1._.mine = f32[8,1024]{1,0:T(8,128)S(1)} custom-call(s32[2,24]{1,0:T(2,128)S(1)} %pad_add_fusion.table, bf16[2,128,1024]{2,1,0:T(8,128)(2,1)S(1)} %get-tuple-element.23.q_t, bf16[2,128,1024]{2,1,0:T(8,128)(2,1)S(1)} %get-tuple-element.24.c_t, bf16[2,8,2,128,128]{4,3,2,1,0:T(8,128)(2,1)S(1)} %constant_dynamic-update-slice_fusion.near), custom_call_target="tpu_custom_call" | custom-call | flops 1073741824 | bytes 2097152 | tf_op jit(solution)/shard_map/backward_stats/pallas_call | solution.py:337
  35.4 3.7 %collective-permute-start.6 = (f32[8,1024]{1,0:T(8,128)S(1)}, f32[8,1024]{1,0:T(8,128)S(1)}, u32[]{:S(2)}, u32[]{:S(2)}) collective-permute-start(f32[8,1024]{1,0:T(8,128)S(1)} %backward_stats.1._.mine), channel_id=1, source_target_pairs={{0,64},{8,72},{16,80},{24,88},{32,96},{40,104},{48,112},{56,120},{... | collective-permute-start | bytes 98312 | tf_op jit(solution)/shard_map/ppermute | solution.py:357
  39.1 0.0 collective-permute-done.7.q_far
  39.1 3.0 %forward.1 = (bf16[1,144,1024]{2,1,0:T(8,128)(2,1)S(1)}, bf16[1,144,1024]{2,1,0:T(8,128)(2,1)S(1)}) custom-call(s32[2,24]{1,0:T(2,128)S(1)} %pad_add_fusion.table, bf16[1,128,1024]{2,1,0:T(8,128)(2,1)S(1)} %copy-done.2, bf16[1,128,1024]{2,1,0:T(8,128)(2,1)S(1)} %collective-permute-done.7.q_far, ...), custom_call_target="tpu_custom_call" | custom-call | flops 6442450944 | bytes 2097152 | tf_op jit(solution)/shard_map/forward/pallas_call | solution.py:337
  42.1 0.1 collective-permute-start.11
  42.2 0.7 collective-permute-start.10
  42.9 0.0 collective-permute-done.6.other
  42.9 2.5 %backward_grads.1 = (bf16[1,128,1024]{2,1,0:T(8,128)(2,1)S(1)}, bf16[1,128,1024]{2,1,0:T(8,128)(2,1)S(1)}, bf16[3,2,128,128]{3,2,1,0:T(8,128)(2,1)S(1)}, bf16[3,...) custom-call(s32[2,24]{1,0:T(2,128)S(1)} %pad_add_fusion.table, bf16[2,128,1024]{2,1,0:T(8,128)(2,1)S(1)} %get-tuple-element.23.q_t, ...), custom_call_target="tpu_custom_call" | custom-call | flops 21474836480 | bytes 2097152 | tf_op jit(solution)/shard_map/backward_grads/pallas_call | solution.py:337
  45.4 2.0 %collective-permute-start.12 = (bf16[3,2,128,128]{3,2,1,0:T(8,128)(2,1)S(1)}, bf16[3,2,128,128]{3,2,1,0:T(8,128)(2,1)S(1)}, u32[]{:S(2)}, u32[]{:S(2)}) collective-permute-start(bf16[3,2,128,128]{3,2,1,0:T(8,128)(2,1)S(1)} %get-tuple-element.35), channel_id=1, source_target_pairs={{0,56},{8,0},{16,8},{24,16},{32,24},{40,32},{48,40},{56,48},{64,12... | collective-permute-start | bytes 589832 | tf_op jit(solution)/shard_map/ppermute | solution.py:353
  47.4 0.1 collective-permute-start.13
  47.5 1.9 %collective-permute-start.8 = (bf16[1,128,1024]{2,1,0:T(8,128)(2,1)S(1)}, bf16[1,128,1024]{2,1,0:T(8,128)(2,1)S(1)}, u32[]{:S(2)}, u32[]{:S(2)}) collective-permute-start(bf16[1,128,1024]{2,1,0:T(8,128)(2,1)S(1)} %get-tuple-element.29), channel_id=1, source_target_pairs={{0,128},{8,136},{16,144},{24,152},{32,160},{40,168},{48,176},{56,1... | collective-permute-start | bytes 786440 | tf_op jit(solution)/shard_map/ppermute | solution.py:366
  49.4 4.2 %collective-permute-done.13.high = bf16[2,2,128,128]{3,2,1,0:T(8,128)(2,1)S(1)} collective-permute-done((bf16[2,2,128,128]{3,2,1,0:T(8,128)(2,1)S(1)}, bf16[2,2,128,128]{3,2,1,0:T(8,128)(2,1)S(1)}, u32[]{:S(2)}, u32[]{:S(2)}) %collective-permute-start.13) | collective-permute-done | bytes 131104 | tf_op jit(solution)/shard_map/ppermute | solution.py:353
  53.5 1.6 %collective-permute-start.9 = (bf16[1,128,1024]{2,1,0:T(8,128)(2,1)S(1)}, bf16[1,128,1024]{2,1,0:T(8,128)(2,1)S(1)}, u32[]{:S(2)}, u32[]{:S(2)}) collective-permute-start(bf16[1,128,1024]{2,1,0:T(8,128)(2,1)S(1)} %get-tuple-element.30), channel_id=1, source_target_pairs={{0,192},{8,200},{16,208},{24,216},{32,224},{40,232},{48,240},{56,2... | collective-permute-start | bytes 786440 | tf_op jit(solution)/shard_map/ppermute | solution.py:366
  55.1 0.0 collective-permute-done.12.low
  55.1 0.0 collective-permute-done.11.b._b
  55.1 0.0 collective-permute-done.10.a._a
  55.1 0.1 add.3
  55.2 1.5 %collective-permute-start.14 = (bf16[2,128,128]{2,1,0:T(8,128)(2,1)S(1)}, bf16[2,128,128]{2,1,0:T(8,128)(2,1)S(1)}, u32[]{:S(2)}, u32[]{:S(2)}) collective-permute-start(bf16[2,128,128]{2,1,0:T(8,128)(2,1)S(1)} %get-tuple-element.37), channel_id=1, source_target_pairs={{0,128},{8,136},{16,144},{24,152},{32,160},{40,168},{48,176},{56,1... | collective-permute-start | bytes 196616 | tf_op jit(solution)/shard_map/ppermute | solution.py:366
  56.7 1.5 %collective-permute-start.15 = (bf16[2,128,128]{2,1,0:T(8,128)(2,1)S(1)}, bf16[2,128,128]{2,1,0:T(8,128)(2,1)S(1)}, u32[]{:S(2)}, u32[]{:S(2)}) collective-permute-start(bf16[2,128,128]{2,1,0:T(8,128)(2,1)S(1)} %get-tuple-element.38), channel_id=1, source_target_pairs={{0,168},{8,176},{16,184},{24,128},{32,136},{40,144},{48,152},{56,1... | collective-permute-start | bytes 196616 | tf_op jit(solution)/shard_map/ppermute | solution.py:366
  58.2 3.2 %collective-permute-start.16 = (bf16[2,128,128]{2,1,0:T(8,128)(2,1)S(1)}, bf16[2,128,128]{2,1,0:T(8,128)(2,1)S(1)}, u32[]{:S(2)}, u32[]{:S(2)}) collective-permute-start(bf16[2,128,128]{2,1,0:T(8,128)(2,1)S(1)} %get-tuple-element.39), channel_id=1, source_target_pairs={{0,152},{8,160},{16,168},{24,176},{32,184},{40,128},{48,136},{56,1... | collective-permute-start | bytes 196616 | tf_op jit(solution)/shard_map/ppermute | solution.py:366
  61.4 0.0 collective-permute-done.8.dq
  61.4 0.0 collective-permute-done.9.dq_far
  61.4 1.2 %finish.1 = (bf16[1,128,1024]{2,1,0:T(8,128)(2,1)}, bf16[1,128,1024]{2,1,0:T(8,128)(2,1)}, f32[8,128]{1,0:T(8,128)S(1)}) custom-call(bf16[1,128,1024]{2,1,0:T(8,128)(2,1)S(1)} %collective-permute-done.8.dq, bf16[1,128,1024]{2,1,0:T(8,128)(2,1)S(1)} %collective-permute-done.9.dq_far, bf16[1,144,1024]{2,1,0:T(8,128)(2,1)S(1)} %collective-permute-done.10.a._a, ...), custom_call_target="tpu_custom_call" | custom-call | flops 2147483648 | bytes 2097152 | tf_op jit(solution)/shard_map/finish/pallas_call | solution.py:337
  62.6 0.0 collective-permute-done.14.own
  62.6 1.0 %collective-permute-done.15.below = bf16[2,128,128]{2,1,0:T(8,128)(2,1)S(1)} collective-permute-done((bf16[2,128,128]{2,1,0:T(8,128)(2,1)S(1)}, bf16[2,128,128]{2,1,0:T(8,128)(2,1)S(1)}, u32[]{:S(2)}, u32[]{:S(2)}) %collective-permute-start.15) | collective-permute-done | bytes 65568 | tf_op jit(solution)/shard_map/ppermute | solution.py:366
  63.6 2.7 %collective-permute-done.16.above = bf16[2,128,128]{2,1,0:T(8,128)(2,1)S(1)} collective-permute-done((bf16[2,128,128]{2,1,0:T(8,128)(2,1)S(1)}, bf16[2,128,128]{2,1,0:T(8,128)(2,1)S(1)}, u32[]{:S(2)}, u32[]{:S(2)}) %collective-permute-start.16) | collective-permute-done | bytes 65568 | tf_op jit(solution)/shard_map/ppermute | solution.py:366
  66.4 0.7 total.1
  (9 shorter events, 0.1 us)
Async XLA Ops:
  0.6 10.8 %copy-start = (bf16[1,128,1024]{2,1,0:T(8,128)(2,1)S(1)}, bf16[1,128,1024]{2,1,0:T(8,128)(2,1)}, u32[]{:S(2)}) copy-start(bf16[1,128,1024]{2,1,0:T(8,128)(2,1)} %q.2) | copy-start | bytes 786436
  0.6 14.3 %copy-start.3 = (s32[2,8]{1,0:T(2,128)S(1)}, s32[2,8]{1,0:T(2,128)}, u32[]{:S(2)}) copy-start(s32[2,8]{1,0:T(2,128)} %param.12) | copy-start | bytes 196
  0.7 14.3 %copy-start.4 = (s32[2,16]{1,0:T(2,128)S(1)}, s32[2,16]{1,0:T(2,128)}, u32[]{:S(2)}) copy-start(s32[2,16]{1,0:T(2,128)} %param.13) | copy-start | bytes 388
  1.6 15.2 %collective-permute-start.3 = (bf16[2,1,2,128,128]{4,3,2,1,0:T(8,128)(2,1)S(1)}, bf16[2,1,2,128,128]{4,3,2,1,0:T(8,128)(2,1)S(1)}, u32[]{:S(2)}, u32[]{:S(2)}) collective-permute-start(bf16[2,1,2,128,128]{4,3,2,1,0:T(8,128)(2,1)S(1)} %pad_maximum_fusion.x), channel_id=1, source_target_pairs={{0,40},{8,48},{16,56},{24,0},{32,8},{40,16},{48,24},{56,32},{64,10... | collective-permute-start | bytes 393224 | tf_op jit(solution)/shard_map/ppermute | solution.py:353
  8.4 12.9 %collective-permute-start.2 = (bf16[2,1,2,128,128]{4,3,2,1,0:T(8,128)(2,1)S(1)}, bf16[2,1,2,128,128]{4,3,2,1,0:T(8,128)(2,1)S(1)}, u32[]{:S(2)}, u32[]{:S(2)}) collective-permute-start(bf16[2,1,2,128,128]{4,3,2,1,0:T(8,128)(2,1)S(1)} %pad_maximum_fusion.x), channel_id=1, source_target_pairs={{0,24},{8,32},{16,40},{24,48},{32,56},{40,0},{48,8},{56,16},{64,88... | collective-permute-start | bytes 393224 | tf_op jit(solution)/shard_map/ppermute | solution.py:353
  8.4 30.7 %collective-permute-start.7 = (bf16[1,128,1024]{2,1,0:T(8,128)(2,1)}, bf16[1,128,1024]{2,1,0:T(8,128)(2,1)S(1)}, u32[]{:S(2)}, u32[]{:S(2)}) collective-permute-start(bf16[1,128,1024]{2,1,0:T(8,128)(2,1)} %q.3), channel_id=1, source_target_pairs={{0,64},{8,72},{16,80},{24,88},{32,96},{40,104},{48,112},{56,120},{... | collective-permute-start | bytes 786440 | tf_op jit(solution)/shard_map/ppermute | solution.py:357
  11.4 13.5 %collective-permute-start = (bf16[1,128,1024]{2,1,0:T(8,128)(2,1)S(1)}, bf16[1,128,1024]{2,1,0:T(8,128)(2,1)S(1)}, u32[]{:S(2)}, u32[]{:S(2)}) collective-permute-start(bf16[1,128,1024]{2,1,0:T(8,128)(2,1)S(1)} %copy-done), channel_id=1, source_target_pairs={{0,64},{8,72},{16,80},{24,88},{32,96},{40,104},{48,112},{56,120},{... | collective-permute-start | bytes 786440 | tf_op jit(solution)/shard_map/ppermute | solution.py:357
  11.9 17.2 %collective-permute-start.1 = (bf16[1,128,1024]{2,1,0:T(8,128)(2,1)}, bf16[1,128,1024]{2,1,0:T(8,128)(2,1)S(1)}, u32[]{:S(2)}, u32[]{:S(2)}) collective-permute-start(bf16[1,128,1024]{2,1,0:T(8,128)(2,1)} %c.1), channel_id=1, source_target_pairs={{0,64},{8,72},{16,80},{24,88},{32,96},{40,104},{48,112},{56,120},{... | collective-permute-start | bytes 786440 | tf_op jit(solution)/shard_map/ppermute | solution.py:357
  21.4 12.0 %collective-permute-start.5 = (bf16[2,2,2,128,128]{4,3,2,1,0:T(8,128)(2,1)S(1)}, bf16[2,2,2,128,128]{4,3,2,1,0:T(8,128)(2,1)S(1)}, u32[]{:S(2)}, u32[]{:S(2)}) collective-permute-start(bf16[2,2,2,128,128]{4,3,2,1,0:T(8,128)(2,1)S(1)} %get-tuple-element.27), channel_id=1, source_target_pairs={{0,56},{8,0},{16,8},{24,16},{32,24},{40,32},{48,40},{56,48},{64,12... | collective-permute-start | bytes 786440 | tf_op jit(solution)/shard_map/ppermute | solution.py:353
  21.5 7.6 %copy-start.1 = (bf16[1,128,1024]{2,1,0:T(8,128)(2,1)S(1)}, bf16[1,128,1024]{2,1,0:T(8,128)(2,1)}, u32[]{:S(2)}) copy-start(bf16[1,128,1024]{2,1,0:T(8,128)(2,1)} %c.1) | copy-start | bytes 786436
  21.5 11.8 %collective-permute-start.4 = (bf16[2,3,2,128,128]{4,3,2,1,0:T(8,128)(2,1)S(1)}, bf16[2,3,2,128,128]{4,3,2,1,0:T(8,128)(2,1)S(1)}, u32[]{:S(2)}, u32[]{:S(2)}) collective-permute-start(bf16[2,3,2,128,128]{4,3,2,1,0:T(8,128)(2,1)S(1)} %get-tuple-element.22._), channel_id=1, source_target_pairs={{0,8},{8,16},{16,24},{24,32},{32,40},{40,48},{48,56},{56,0},{64,72... | collective-permute-start | bytes 1179656 | tf_op jit(solution)/shard_map/ppermute | solution.py:353
  33.4 5.7 %copy-start.2 = (bf16[1,128,1024]{2,1,0:T(8,128)(2,1)S(1)}, bf16[1,128,1024]{2,1,0:T(8,128)(2,1)}, u32[]{:S(2)}) copy-start(bf16[1,128,1024]{2,1,0:T(8,128)(2,1)} %q.3) | copy-start | bytes 786436
  35.4 7.5 %collective-permute-start.6 = (f32[8,1024]{1,0:T(8,128)S(1)}, f32[8,1024]{1,0:T(8,128)S(1)}, u32[]{:S(2)}, u32[]{:S(2)}) collective-permute-start(f32[8,1024]{1,0:T(8,128)S(1)} %backward_stats.1._.mine), channel_id=1, source_target_pairs={{0,64},{8,72},{16,80},{24,88},{32,96},{40,104},{48,112},{56,120},{... | collective-permute-start | bytes 98312 | tf_op jit(solution)/shard_map/ppermute | solution.py:357
  42.1 13.0 %collective-permute-start.11 = (bf16[1,144,1024]{2,1,0:T(8,128)(2,1)S(1)}, bf16[1,144,1024]{2,1,0:T(8,128)(2,1)S(1)}, u32[]{:S(2)}, u32[]{:S(2)}) collective-permute-start(bf16[1,144,1024]{2,1,0:T(8,128)(2,1)S(1)} %get-tuple-element.31), channel_id=1, source_target_pairs={{0,192},{8,200},{16,208},{24,216},{32,224},{40,232},{48,240},{56,2... | collective-permute-start | bytes 884744 | tf_op jit(solution)/shard_map/ppermute | solution.py:366
  42.2 12.9 %collective-permute-start.10 = (bf16[1,144,1024]{2,1,0:T(8,128)(2,1)S(1)}, bf16[1,144,1024]{2,1,0:T(8,128)(2,1)S(1)}, u32[]{:S(2)}, u32[]{:S(2)}) collective-permute-start(bf16[1,144,1024]{2,1,0:T(8,128)(2,1)S(1)} %get-tuple-element.28._), channel_id=1, source_target_pairs={{0,128},{8,136},{16,144},{24,152},{32,160},{40,168},{48,176},{56,1... | collective-permute-start | bytes 884744 | tf_op jit(solution)/shard_map/ppermute | solution.py:366
  45.4 9.7 %collective-permute-start.12 = (bf16[3,2,128,128]{3,2,1,0:T(8,128)(2,1)S(1)}, bf16[3,2,128,128]{3,2,1,0:T(8,128)(2,1)S(1)}, u32[]{:S(2)}, u32[]{:S(2)}) collective-permute-start(bf16[3,2,128,128]{3,2,1,0:T(8,128)(2,1)S(1)} %get-tuple-element.35), channel_id=1, source_target_pairs={{0,56},{8,0},{16,8},{24,16},{32,24},{40,32},{48,40},{56,48},{64,12... | collective-permute-start | bytes 589832 | tf_op jit(solution)/shard_map/ppermute | solution.py:353
  47.4 6.2 %collective-permute-start.13 = (bf16[2,2,128,128]{3,2,1,0:T(8,128)(2,1)S(1)}, bf16[2,2,128,128]{3,2,1,0:T(8,128)(2,1)S(1)}, u32[]{:S(2)}, u32[]{:S(2)}) collective-permute-start(bf16[2,2,128,128]{3,2,1,0:T(8,128)(2,1)S(1)} %get-tuple-element.36), channel_id=1, source_target_pairs={{0,8},{8,16},{16,24},{24,32},{32,40},{40,48},{48,56},{56,0},{64,72... | collective-permute-start | bytes 393224 | tf_op jit(solution)/shard_map/ppermute | solution.py:353
  47.5 13.9 %collective-permute-start.8 = (bf16[1,128,1024]{2,1,0:T(8,128)(2,1)S(1)}, bf16[1,128,1024]{2,1,0:T(8,128)(2,1)S(1)}, u32[]{:S(2)}, u32[]{:S(2)}) collective-permute-start(bf16[1,128,1024]{2,1,0:T(8,128)(2,1)S(1)} %get-tuple-element.29), channel_id=1, source_target_pairs={{0,128},{8,136},{16,144},{24,152},{32,160},{40,168},{48,176},{56,1... | collective-permute-start | bytes 786440 | tf_op jit(solution)/shard_map/ppermute | solution.py:366
  53.5 7.9 %collective-permute-start.9 = (bf16[1,128,1024]{2,1,0:T(8,128)(2,1)S(1)}, bf16[1,128,1024]{2,1,0:T(8,128)(2,1)S(1)}, u32[]{:S(2)}, u32[]{:S(2)}) collective-permute-start(bf16[1,128,1024]{2,1,0:T(8,128)(2,1)S(1)} %get-tuple-element.30), channel_id=1, source_target_pairs={{0,192},{8,200},{16,208},{24,216},{32,224},{40,232},{48,240},{56,2... | collective-permute-start | bytes 786440 | tf_op jit(solution)/shard_map/ppermute | solution.py:366
  55.2 7.4 %collective-permute-start.14 = (bf16[2,128,128]{2,1,0:T(8,128)(2,1)S(1)}, bf16[2,128,128]{2,1,0:T(8,128)(2,1)S(1)}, u32[]{:S(2)}, u32[]{:S(2)}) collective-permute-start(bf16[2,128,128]{2,1,0:T(8,128)(2,1)S(1)} %get-tuple-element.37), channel_id=1, source_target_pairs={{0,128},{8,136},{16,144},{24,152},{32,160},{40,168},{48,176},{56,1... | collective-permute-start | bytes 196616 | tf_op jit(solution)/shard_map/ppermute | solution.py:366
  56.7 7.0 %collective-permute-start.15 = (bf16[2,128,128]{2,1,0:T(8,128)(2,1)S(1)}, bf16[2,128,128]{2,1,0:T(8,128)(2,1)S(1)}, u32[]{:S(2)}, u32[]{:S(2)}) collective-permute-start(bf16[2,128,128]{2,1,0:T(8,128)(2,1)S(1)} %get-tuple-element.38), channel_id=1, source_target_pairs={{0,168},{8,176},{16,184},{24,128},{32,136},{40,144},{48,152},{56,1... | collective-permute-start | bytes 196616 | tf_op jit(solution)/shard_map/ppermute | solution.py:366
  58.2 8.2 %collective-permute-start.16 = (bf16[2,128,128]{2,1,0:T(8,128)(2,1)S(1)}, bf16[2,128,128]{2,1,0:T(8,128)(2,1)S(1)}, u32[]{:S(2)}, u32[]{:S(2)}) collective-permute-start(bf16[2,128,128]{2,1,0:T(8,128)(2,1)S(1)} %get-tuple-element.39), channel_id=1, source_target_pairs={{0,152},{8,160},{16,168},{24,176},{32,184},{40,128},{48,136},{56,1... | collective-permute-start | bytes 196616 | tf_op jit(solution)/shard_map/ppermute | solution.py:366
